TPU v7x, 32 devices: a whole 2x2x4 slice. The times are simulated.
32 devices in a mesh: shard: 4 (over y, x), ctx: 4 (over z), tp: 2 (over core).
Axes of the slice: x: 2, y: 2, z: 4, core: 2. Of those that a mesh axis runs over, the one named last changes fastest.
Arguments:
- tokens: bfloat16 [8192, 1024], P(('shard', 'ctx')), may hold values from -6 to 6
- segment: int32 [8192], P('shard'), may hold values from 0 to 4, as said below
- gain_attn: bfloat16 [1024], P('shard'), may hold values from 0.5 to 1.5
- w_query: bfloat16 [1024, 512], P('shard', 'tp'), may hold values from -0.1875 to 0.1875
- key_value_weight: bfloat16 [1024, 256], P('shard', 'tp'), may hold values from -0.1875 to 0.1875
- w_attn_out: bfloat16 [512, 1024], P('tp', 'shard'), may hold values from -1 to 1
- w_gate_z: bfloat16 [1024, 1536], P('shard', 'tp'), may hold values from -0.1875 to 0.1875
- w_ssm_in: bfloat16 [1024, 1536], P('shard', 'tp'), may hold values from -0.1875 to 0.1875
- w_step: bfloat16 [1024, 24], P('shard', 'tp'), may hold values from -0.1875 to 0.1875
- w_bc: bfloat16 [1024, 256], P('shard'), may hold values from -0.1875 to 0.1875
- w_conv_x: float32 [4, 1536], P(None, 'tp'), may hold values from -0.5 to 0.5
- conv_x_bias: float32 [1536], P('tp'), may hold values from -0.5 to 0.5
- w_conv_bc: float32 [4, 256], replicated, may hold values from -0.5 to 0.5
- conv_bc_bias: float32 [256], replicated, may hold values from -0.5 to 0.5
- step_bias: float32 [24], P('tp'), may hold values from -4 to -1
- decay_log: float32 [24], P('tp'), may hold values from -7 to -1.5
- skip_gain: float32 [24], P('tp'), may hold values from 0.5 to 1.5
- w_ssm_out: bfloat16 [1536, 1024], P('tp', 'shard'), may hold values from -0.01953125 to 0.01953125
- gain_ffn: bfloat16 [1024], P('shard'), may hold values from 0.5 to 1.5
- w_gate: bfloat16 [1024, 2048], P('shard', 'tp'), may hold values from -0.1875 to 0.1875
- w_up: bfloat16 [1024, 2048], P('shard', 'tp'), may hold values from -0.1875 to 0.1875
- w_down: bfloat16 [2048, 1024], P('tp', 'shard'), may hold values from -0.125 to 0.125
- grad_out: bfloat16 [8192, 1024], P(('shard', 'ctx')), may hold values from -6 to 6
Outputs:
- result: bfloat16 [8192, 1024], P(('shard', 'ctx'))
- grad_tokens: bfloat16 [8192, 1024], P(('shard', 'ctx'))
- grad_gain_attn: float32 [1024], P('shard')
- grad_w_query: float32 [1024, 512], P('shard', 'tp')
- grad_w_keyval: float32 [1024, 256], P('shard', 'tp')
- grad_w_attn_out: float32 [512, 1024], P('tp', 'shard')
- grad_w_gate_z: float32 [1024, 1536], P('shard', 'tp')
- grad_w_ssm_in: float32 [1024, 1536], P('shard', 'tp')
- grad_w_step: float32 [1024, 24], P('shard', 'tp')
- grad_w_bc: float32 [1024, 256], P('shard')
- grad_w_conv_x: float32 [4, 1536], P(None, 'tp')
- grad_conv_x_bias: float32 [1536], P('tp')
- grad_w_conv_bc: float32 [4, 256], replicated
- grad_conv_bc_bias: float32 [256], replicated
- grad_step_bias: float32 [24], P('tp')
- grad_decay_log: float32 [24], P('tp')
- grad_skip_gain: float32 [24], P('tp')
- grad_w_ssm_out: float32 [1536, 1024], P('tp', 'shard')
- grad_gain_ffn: float32 [1024], P('shard')
- grad_w_gate: float32 [1024, 2048], P('shard', 'tp')
- grad_w_up: float32 [1024, 2048], P('shard', 'tp')
- grad_w_down: float32 [2048, 1024], P('tp', 'shard')
Inputs may be any that keep to these rules, and one draw needn't show every extreme that they name: `segment`: within each aligned run of 2048 tokens (one group) the numbers never fall and the last token has 4; one sequence of each group has 64 or more tokens among the group's first 512 and among its last 512.
All inputs are finite; a program needn't handle non-finite values.
Results may differ from a plain program's by a relative error of at most 0.024.
Values may be sent and summed in bfloat16 or wider, within the bound.
A program may use at most 192 MiB of HBM per device.

v0:
```python
from functools import partial

import jax
import jax.numpy as jnp
from jax import lax
from jax.sharding import PartitionSpec as P

HEAD_SIZE = 64
MP = 64
NS = 128
SPAN = 128
TAPS = 4


HIGHEST = lax.Precision.HIGHEST
ROPE_BASE = 100000000000.0


def carried_in(shard, axis, combine, identity):
    length, position = (lax.axis_size(axis), lax.axis_index(axis))
    everything = jax.tree.map(
        lambda part, kind: lax.all_gather(part.astype(kind), axis),
        shard,
        (jnp.bfloat16, jnp.bfloat16),
    )
    start = jax.tree.map(
        lambda part, zero: jnp.broadcast_to(jnp.asarray(zero, part.dtype), part.shape),
        shard,
        identity,
    )

    def turn(k, before):
        reached = k < position
        new = combine(
            before, jax.tree.map(lambda part, own: part[k].astype(own.dtype), everything, shard)
        )
        return jax.tree.map(lambda a, b: jnp.where(reached, a, b), new, before)

    return lax.fori_loop(0, length, turn, start)


def carried_in_2(shard, axis, join, neutral):
    count = lax.axis_size(axis)
    place = lax.axis_index(axis)
    ahead = count - 1 - place
    gathered = jax.tree.map(
        lambda a, kind: lax.all_gather(a.astype(kind), axis),
        shard,
        jax.tree.map(lambda a: jnp.bfloat16 if a.dtype == jnp.float32 else a.dtype, shard),
    )
    state = jax.tree.map(lambda a, e: jnp.zeros_like(a) + jnp.asarray(e, a.dtype), shard, neutral)

    def one(turn, state):
        source = count - 1 - turn
        return join(
            state,
            jax.tree.map(
                lambda a, own: lax.dynamic_index_in_dim(a, source, 0, False).astype(own.dtype),
                gathered,
                shard,
            ),
        )

    return lax.fori_loop(0, ahead, one, state)


def rms_scale(values):
    return lax.rsqrt(jnp.mean(values * values, axis=-1, keepdims=True) + 1e-05)


def norm_back(values, scale, gain, d_normed):
    scaled = d_normed * gain[None, :]
    d_values = scale * scaled - values * scale**3 * jnp.mean(
        scaled * values, axis=-1, keepdims=True
    )
    return (d_values, jnp.sum(d_normed * values * scale, axis=0))


def contract_rows(former, latter):
    return lax.dot_general(
        former, latter, (((0,), (0,)), ((), ())), preferred_element_type=jnp.float32
    )


def contract_cols(former, latter):
    return lax.dot_general(
        former, latter, (((1,), (1,)), ((), ())), preferred_element_type=jnp.float32
    )


def silu_slope(values):
    sigma = jax.nn.sigmoid(values)
    return sigma * (1.0 + values * (1.0 - sigma))


def positions_in_group(segments):
    count = segments.shape[0]
    index = jnp.arange(count, dtype=jnp.int32)
    fresh = jnp.concatenate([jnp.ones((1,), bool), segments[1:] != segments[:-1]])
    starts = lax.cummax(jnp.where(fresh, index, 0), axis=0)
    return index - starts


def rope_tables(positions):
    exponents = jnp.arange(0, HEAD_SIZE, 2, dtype=jnp.float32) / HEAD_SIZE
    frequency = ROPE_BASE ** (-exponents)
    angle = positions.astype(jnp.float32)[:, None] * frequency[None, :]
    cosine = jnp.cos(angle)
    sine = jnp.sin(angle)
    return (jnp.concatenate([cosine, cosine], axis=-1), jnp.concatenate([sine, sine], axis=-1))


def rotate(values, cosine, sine):
    half = values.shape[-1] // 2
    turned = jnp.concatenate([-values[..., half:], values[..., :half]], axis=-1)
    return values * cosine + turned * sine


def conv_silu(extended, taps, bias, seg_ext):
    reach = taps.shape[0] - 1
    packed_length = extended.shape[0] - reach
    current = seg_ext[reach:]
    total = jnp.zeros((packed_length, extended.shape[1]), jnp.float32) + bias[None, :]
    for delay in range(taps.shape[0]):
        source = extended[reach - delay : reach - delay + packed_length]
        same = (seg_ext[reach - delay : reach - delay + packed_length] == current)[:, None]
        total = total + jnp.where(same, taps[delay][None, :] * source, 0.0)
    return jax.nn.silu(total)


def span_step(decay_rates, carried, block_in):
    states, seg_last = carried
    x_block, b_block, c_block, step_block, seg_block = block_in
    cumulative = jnp.cumsum(step_block * decay_rates[None, :], axis=0)
    packed_length = seg_block.shape[0]
    position = jnp.arange(packed_length)
    causal = (position[:, None] >= position[None, :]) & (seg_block[:, None] == seg_block[None, :])
    spread = cumulative[:, None, :] - cumulative[None, :, :]
    decays = jnp.where(causal[:, :, None], jnp.exp(jnp.minimum(spread, 0.0)), 0.0)
    intersection = jnp.dot(c_block, b_block.T, precision=HIGHEST)
    weighted = intersection[:, :, None] * decays
    inflow = step_block[:, :, None] * x_block
    outputs = jnp.einsum("tuh,uhp->thp", weighted, inflow, precision=HIGHEST)
    carry_in = jnp.where((seg_block == seg_last)[:, None], jnp.exp(cumulative), 0.0)
    outputs = outputs + carry_in[:, :, None] * jnp.einsum(
        "tn,hpn->thp", c_block, states, precision=HIGHEST
    )
    ending = jnp.where(
        (seg_block == seg_block[-1])[:, None], jnp.exp(cumulative[-1][None, :] - cumulative), 0.0
    )
    keep_all = jnp.where(seg_block[-1] == seg_last, jnp.exp(cumulative[-1]), 0.0)
    states = keep_all[:, None, None] * states + jnp.einsum(
        "uh,uhp,un->hpn", ending, inflow, b_block, precision=HIGHEST
    )
    return ((states, seg_block[-1]), outputs)


def ssm_local(inputs, b_values, c_values, steps, decay_log, seg_local, seg_before):
    decay_rates = -jnp.exp(decay_log)
    packed_length = inputs.shape[0]
    blocks = packed_length // SPAN
    head_count = decay_log.shape[0]

    def to_blocks(values):
        return values.reshape((blocks, SPAN) + values.shape[1:])

    initial = (jnp.zeros((head_count, MP, NS), jnp.float32), seg_before)
    (final_state, seg_end), outputs = lax.scan(
        partial(span_step, decay_rates),
        initial,
        (
            to_blocks(inputs),
            to_blocks(b_values),
            to_blocks(c_values),
            to_blocks(steps),
            to_blocks(seg_local),
        ),
    )
    through = jnp.where(
        seg_local[-1] == seg_before, jnp.exp(jnp.sum(steps * decay_rates[None, :], axis=0)), 0.0
    )
    return (outputs.reshape(inputs.shape), through, final_state)


def ssm_inflow(steps, decay_log, c_values, state_in, seg_local, seg_before):
    cumulative = jnp.cumsum(steps * (-jnp.exp(decay_log))[None, :], axis=0)
    carry_in = jnp.where((seg_local == seg_before)[:, None], jnp.exp(cumulative), 0.0)
    return carry_in[:, :, None] * jnp.einsum("tn,hpn->thp", c_values, state_in, precision=HIGHEST)


def combine_states(earlier, later):
    return (earlier[0] * later[0], earlier[1] * later[0][:, None, None] + later[1])


def local(
    tokens,
    segment,
    gain_attn,
    w_query,
    key_value_weight,
    w_attn_out,
    w_gate_z,
    w_ssm_in,
    w_step,
    w_bc,
    w_conv_x,
    conv_x_bias,
    w_conv_bc,
    conv_bc_bias,
    step_bias,
    decay_log,
    skip_gain,
    w_ssm_out,
    gain_ffn,
    w_gate,
    w_up,
    w_down,
    grad_out,
):
    gathered = (
        lax.all_gather(gain_attn, "shard", axis=0, tiled=True),
        lax.all_gather(w_query, "shard", axis=0, tiled=True),
        lax.all_gather(key_value_weight, "shard", axis=0, tiled=True),
        lax.all_gather(w_attn_out, "shard", axis=1, tiled=True),
        lax.all_gather(w_gate_z, "shard", axis=0, tiled=True),
        lax.all_gather(w_ssm_in, "shard", axis=0, tiled=True),
        lax.all_gather(w_step, "shard", axis=0, tiled=True),
        lax.all_gather(w_bc, "shard", axis=0, tiled=True),
        lax.all_gather(w_ssm_out, "shard", axis=1, tiled=True),
        lax.all_gather(gain_ffn, "shard", axis=0, tiled=True),
        lax.all_gather(w_gate, "shard", axis=0, tiled=True),
        lax.all_gather(w_up, "shard", axis=0, tiled=True),
        lax.all_gather(w_down, "shard", axis=1, tiled=True),
    )
    (
        full_gain_attn,
        full_query,
        full_keyval,
        full_attn_out,
        full_gate_z,
        full_ssm_in,
        full_step,
        full_bc,
        full_ssm_out,
        full_gain_ffn,
        full_gate,
        full_up,
        full_down,
    ) = gathered
    row_count = tokens.shape[0]
    ctx_rank = lax.axis_index("ctx")
    ctx_count = lax.axis_size("ctx")
    first_row = ctx_rank * row_count
    seg_local = lax.dynamic_slice_in_dim(segment, first_row, row_count)
    seg_before = jnp.where(
        ctx_rank > 0, lax.dynamic_slice_in_dim(segment, jnp.maximum(first_row - 1, 0), 1)[0], -1
    )
    query_pos = first_row + jnp.arange(row_count)
    scaling = HEAD_SIZE ** (-0.5)
    reach = TAPS - 1
    lower = jnp.maximum(ctx_rank - 1, 0) * reach
    positions = lax.dynamic_slice_in_dim(positions_in_group(segment), first_row, row_count)
    cosine, sine = rope_tables(positions)
    seg_padded = jnp.concatenate([jnp.full((reach,), -1, jnp.int32), segment])
    seg_ext = lax.dynamic_slice_in_dim(seg_padded, first_row, row_count + reach)
    hidden_in = tokens.astype(jnp.float32)
    gain_one = full_gain_attn.astype(jnp.float32)
    scale_one = rms_scale(hidden_in)
    normalized_input = (hidden_in * scale_one * gain_one[None, :]).astype(jnp.bfloat16)
    query_raw = jnp.dot(normalized_input, full_query, preferred_element_type=jnp.float32)
    head_local = query_raw.shape[1] // HEAD_SIZE
    query_rot = rotate(
        query_raw.reshape(row_count, head_local, HEAD_SIZE), cosine[:, None, :], sine[:, None, :]
    )
    queries = query_rot.reshape(row_count, head_local * HEAD_SIZE).astype(jnp.bfloat16)
    unrotated_key_value = jnp.dot(normalized_input, full_keyval, preferred_element_type=jnp.float32)
    keyval = jnp.concatenate(
        [
            rotate(unrotated_key_value[:, :HEAD_SIZE], cosine, sine),
            unrotated_key_value[:, HEAD_SIZE:],
        ],
        axis=-1,
    ).astype(jnp.bfloat16)
    query_heads = queries.reshape(row_count, head_local, HEAD_SIZE).transpose(1, 0, 2)
    raw_x = jnp.dot(normalized_input, full_ssm_in, preferred_element_type=jnp.float32).astype(
        jnp.bfloat16
    )
    raw_bc = jnp.dot(normalized_input, full_bc, preferred_element_type=jnp.float32).astype(
        jnp.bfloat16
    )
    all_keys, all_tail_x, all_tail_bc = (
        lax.all_gather(keyval, "ctx", axis=0, tiled=True),
        lax.all_gather(raw_x[row_count - reach :], "ctx", axis=0, tiled=True),
        lax.all_gather(raw_bc[row_count - reach :], "ctx", axis=0, tiled=True),
    )
    key_blocks = all_keys.shape[0] // row_count

    def fold_block(carried, block_index):
        row_max, row_total, accum = carried
        start = block_index * row_count
        piece = lax.dynamic_slice_in_dim(all_keys, start, row_count)
        key_seg = lax.dynamic_slice_in_dim(segment, start, row_count)
        key_pos = start + jnp.arange(row_count)
        allowed = (query_pos[:, None] >= key_pos[None, :]) & (
            seg_local[:, None] == key_seg[None, :]
        )
        scores = (
            jnp.einsum(
                "hqd,kd->hqk", query_heads, piece[:, :HEAD_SIZE], preferred_element_type=jnp.float32
            )
            * scaling
        )
        masked = jnp.where(allowed[None], scores, -1e30)
        new_max = jnp.maximum(row_max, jnp.max(masked, axis=-1))
        expon = jnp.where(allowed[None], jnp.exp(masked - new_max[:, :, None]), 0.0)
        factor = jnp.exp(row_max - new_max)
        row_total = row_total * factor + jnp.sum(expon, axis=-1)
        accum = accum * factor[:, :, None] + jnp.einsum(
            "hqk,kd->hqd", expon, piece[:, HEAD_SIZE:].astype(jnp.float32)
        )
        return ((new_max, row_total, accum), None)

    initial = (
        jnp.full((head_local, row_count), -1e30, jnp.float32),
        jnp.zeros((head_local, row_count), jnp.float32),
        jnp.zeros((head_local, row_count, HEAD_SIZE), jnp.float32),
    )
    (row_max, row_total, accum), unused = lax.scan(
        fold_block, initial, jnp.arange(key_blocks, dtype=jnp.int32)
    )
    attn_heads = accum / row_total[:, :, None]
    log_total = row_max + jnp.log(row_total)
    attended = (
        attn_heads.transpose(1, 0, 2)
        .reshape(row_count, head_local * HEAD_SIZE)
        .astype(jnp.bfloat16)
    )
    attn_branch = jnp.dot(attended, full_attn_out, preferred_element_type=jnp.float32)
    ext_x = jnp.concatenate(
        [lax.dynamic_slice_in_dim(all_tail_x, lower, reach), raw_x], axis=0
    ).astype(jnp.float32)
    ext_bc = jnp.concatenate(
        [lax.dynamic_slice_in_dim(all_tail_bc, lower, reach), raw_bc], axis=0
    ).astype(jnp.float32)
    conv_x, conv_x_back = jax.vjp(
        lambda extended, taps, bias: conv_silu(extended, taps, bias, seg_ext),
        ext_x,
        w_conv_x,
        conv_x_bias,
    )
    conv_bc, conv_bc_back = jax.vjp(
        lambda extended, taps, bias: conv_silu(extended, taps, bias, seg_ext),
        ext_bc,
        w_conv_bc,
        conv_bc_bias,
    )
    gate_z = jnp.dot(normalized_input, full_gate_z, preferred_element_type=jnp.float32)
    step_raw = jnp.dot(normalized_input, full_step, preferred_element_type=jnp.float32)
    steps = jax.nn.softplus(step_raw + step_bias[None, :])
    mamba_local = step_bias.shape[0]
    inputs_heads = conv_x.reshape(row_count, mamba_local, MP)
    b_values = conv_bc[:, :NS]
    c_values = conv_bc[:, NS:]
    zero_out, zero_back = jax.vjp(
        lambda inputs, b_part, c_part, step_part, decay_part: ssm_local(
            inputs, b_part, c_part, step_part, decay_part, seg_local, seg_before
        ),
        inputs_heads,
        b_values,
        c_values,
        steps,
        decay_log,
    )
    scanned_zero, through, local_state = zero_out
    through_in, state_in = carried_in(
        (through, local_state),
        "ctx",
        combine_states,
        (jnp.ones_like(through), jnp.zeros_like(local_state)),
    )
    inflow_out, inflow_back = jax.vjp(
        lambda step_part, decay_part, c_part, state_part: ssm_inflow(
            step_part, decay_part, c_part, state_part, seg_local, seg_before
        ),
        steps,
        decay_log,
        c_values,
        state_in,
    )
    scanned = scanned_zero + inflow_out + skip_gain[None, :, None] * inputs_heads
    scanned_flat = scanned.reshape(row_count, mamba_local * MP)
    silu_gate = jax.nn.silu(gate_z)
    gated = (scanned_flat * silu_gate).astype(jnp.bfloat16)
    ssm_branch = jnp.dot(gated, full_ssm_out, preferred_element_type=jnp.float32)
    mixed = lax.psum((attn_branch + ssm_branch).astype(jnp.bfloat16), "tp").astype(jnp.float32)
    middle = hidden_in + mixed
    gain_two = full_gain_ffn.astype(jnp.float32)
    scale_two = rms_scale(middle)
    normed_ffn = (middle * scale_two * gain_two[None, :]).astype(jnp.bfloat16)
    gate_value = jnp.dot(normed_ffn, full_gate, preferred_element_type=jnp.float32)
    up_value = jnp.dot(normed_ffn, full_up, preferred_element_type=jnp.float32)
    active = (jax.nn.silu(gate_value) * up_value).astype(jnp.bfloat16)
    down_part = jnp.dot(active, full_down, preferred_element_type=jnp.float32)
    result = (middle + lax.psum(down_part.astype(jnp.bfloat16), "tp").astype(jnp.float32)).astype(
        jnp.bfloat16
    )
    grad_rows = grad_out.astype(jnp.float32)
    d_active = contract_cols(grad_out, full_down).astype(jnp.bfloat16).astype(jnp.float32)
    grad_down = contract_rows(active, grad_out)
    d_gate = (d_active * up_value * silu_slope(gate_value)).astype(jnp.bfloat16)
    d_up = (d_active * jax.nn.silu(gate_value)).astype(jnp.bfloat16)
    grad_gate = contract_rows(normed_ffn, d_gate)
    grad_up = contract_rows(normed_ffn, d_up)
    d_normed_ffn = lax.psum(
        (contract_cols(d_gate, full_gate) + contract_cols(d_up, full_up)).astype(jnp.bfloat16), "tp"
    ).astype(jnp.float32)
    d_from_ffn, grad_gain_two = norm_back(middle, scale_two, gain_two, d_normed_ffn)
    d_middle = grad_rows + d_from_ffn
    d_mid_low = d_middle.astype(jnp.bfloat16)
    grad_attn_out = contract_rows(attended, d_mid_low)
    d_attended = contract_cols(d_mid_low, full_attn_out).astype(jnp.bfloat16)
    d_att_heads = d_attended.reshape(row_count, head_local, HEAD_SIZE).transpose(1, 0, 2)
    d_att_float = d_att_heads.astype(jnp.float32)
    delta = jnp.sum(d_att_float * attn_heads, axis=-1)

    def key_step(d_query, block_index):
        start = block_index * row_count
        piece = lax.dynamic_slice_in_dim(all_keys, start, row_count)
        key_seg = lax.dynamic_slice_in_dim(segment, start, row_count)
        key_pos = start + jnp.arange(row_count)
        allowed = (query_pos[:, None] >= key_pos[None, :]) & (
            seg_local[:, None] == key_seg[None, :]
        )
        scores = (
            jnp.einsum(
                "hqd,kd->hqk", query_heads, piece[:, :HEAD_SIZE], preferred_element_type=jnp.float32
            )
            * scaling
        )
        weights_soft = jnp.where(
            allowed[None],
            jnp.exp(jnp.where(allowed[None], scores, -1e30) - log_total[:, :, None]),
            0.0,
        )
        d_weights = jnp.einsum(
            "hqd,kd->hqk", d_att_heads, piece[:, HEAD_SIZE:], preferred_element_type=jnp.float32
        )
        d_scores = (weights_soft * (d_weights - delta[:, :, None])).astype(jnp.bfloat16)
        d_query = (
            d_query
            + jnp.einsum(
                "hqk,kd->hqd", d_scores, piece[:, :HEAD_SIZE], preferred_element_type=jnp.float32
            )
            * scaling
        )
        d_keys = (
            jnp.einsum("hqk,hqd->kd", d_scores, query_heads, preferred_element_type=jnp.float32)
            * scaling
        )
        d_values = jnp.einsum("hqk,hqd->kd", weights_soft, d_att_float)
        return (d_query, jnp.concatenate([d_keys, d_values], axis=-1))

    d_query, d_kv_blocks = lax.scan(
        key_step,
        jnp.zeros((head_local, row_count, HEAD_SIZE), jnp.float32),
        jnp.arange(key_blocks, dtype=jnp.int32),
    )
    d_kv_group = d_kv_blocks.reshape(key_blocks * row_count, 2 * HEAD_SIZE)
    grad_ssm_out = contract_rows(gated, d_mid_low)
    d_gated = contract_cols(d_mid_low, full_ssm_out).astype(jnp.bfloat16).astype(jnp.float32)
    d_scanned_flat = d_gated * silu_gate
    d_gate_z = (d_gated * scanned_flat * silu_slope(gate_z)).astype(jnp.bfloat16)
    d_scanned = d_scanned_flat.reshape(row_count, mamba_local, MP)
    grad_skip = jnp.sum(d_scanned * inputs_heads, axis=(0, 2))
    d_steps_in, d_decay_in, d_c_in, d_state_in = inflow_back(d_scanned)
    through_back, state_grad = carried_in_2(
        (through, d_state_in),
        "ctx",
        combine_states,
        (jnp.ones_like(through), jnp.zeros_like(d_state_in)),
    )
    d_through = jnp.sum(state_grad * state_in, axis=(1, 2))
    d_inputs, d_b_values, d_c_zero, d_steps_zero, d_decay_zero = zero_back(
        (d_scanned, d_through, state_grad)
    )
    d_x_post = (d_inputs + skip_gain[None, :, None] * d_scanned).reshape(
        row_count, mamba_local * MP
    )
    d_bc_post = jnp.concatenate([d_b_values, d_c_in + d_c_zero], axis=-1)
    d_ext_x, grad_convx_taps, grad_convx_bias = conv_x_back(d_x_post)
    d_ext_bc, grad_convbc_taps, grad_convbc_bias = conv_bc_back(d_bc_post)
    d_pre = (d_steps_in + d_steps_zero) * jax.nn.sigmoid(step_raw + step_bias[None, :])
    d_step_raw = d_pre.astype(jnp.bfloat16)
    grad_bias = jnp.sum(d_pre, axis=0)
    grad_decay = d_decay_in + d_decay_zero
    send_x = lax.dynamic_update_slice_in_dim(
        jnp.zeros((ctx_count * reach, d_ext_x.shape[1]), jnp.float32), d_ext_x[:reach], lower, 0
    )
    send_bc = lax.dynamic_update_slice_in_dim(
        jnp.zeros((ctx_count * reach, d_ext_bc.shape[1]), jnp.float32), d_ext_bc[:reach], lower, 0
    )
    d_kv_back, tail_x_in, tail_bc_in = (
        lax.psum_scatter(
            d_kv_group.astype(jnp.bfloat16), "ctx", scatter_dimension=0, tiled=True
        ).astype(jnp.float32),
        lax.psum_scatter(
            send_x.astype(jnp.bfloat16), "ctx", scatter_dimension=0, tiled=True
        ).astype(jnp.float32),
        lax.psum_scatter(
            send_bc.astype(jnp.bfloat16), "ctx", scatter_dimension=0, tiled=True
        ).astype(jnp.float32),
    )
    d_keyval = jnp.concatenate(
        [rotate(d_kv_back[:, :HEAD_SIZE], cosine, -sine), d_kv_back[:, HEAD_SIZE:]], axis=-1
    ).astype(jnp.bfloat16)
    d_query_rows = rotate(d_query.transpose(1, 0, 2), cosine[:, None, :], -sine[:, None, :])
    d_queries = d_query_rows.reshape(row_count, head_local * HEAD_SIZE).astype(jnp.bfloat16)
    d_raw_x = d_ext_x[reach:].at[row_count - reach :].add(tail_x_in)
    d_ssm_inputs = d_raw_x.astype(jnp.bfloat16)
    d_bc_raw = d_ext_bc[reach:].at[row_count - reach :].add(tail_bc_in)
    d_normed_part = contract_cols(d_queries, full_query) + contract_cols(d_keyval, full_keyval)
    d_normed_part = (
        d_normed_part
        + contract_cols(d_gate_z, full_gate_z)
        + contract_cols(d_ssm_inputs, full_ssm_in)
        + contract_cols(d_step_raw, full_step)
    )
    d_normed_sum, d_bc_sum = (
        lax.psum(d_normed_part.astype(jnp.bfloat16), "tp").astype(jnp.float32),
        lax.psum(d_bc_raw.astype(jnp.bfloat16), "tp").astype(jnp.float32),
    )
    d_bc_low = d_bc_sum.astype(jnp.bfloat16)
    d_normed = d_normed_sum + contract_cols(d_bc_low, full_bc)
    d_from_attn, grad_gain_one = norm_back(hidden_in, scale_one, gain_one, d_normed)
    grad_tokens = (d_middle + d_from_attn).astype(jnp.bfloat16)
    grad_query = contract_rows(normalized_input, d_queries)
    grad_keyval = contract_rows(normalized_input, d_keyval)
    grad_gate_z = contract_rows(normalized_input, d_gate_z)
    grad_ssm_in = contract_rows(normalized_input, d_ssm_inputs)
    grad_step = contract_rows(normalized_input, d_step_raw)
    grad_bc = contract_rows(normalized_input, d_bc_low)
    weight_grads = (
        grad_gain_one,
        grad_query,
        grad_keyval,
        grad_attn_out,
        grad_gate_z,
        grad_ssm_in,
        grad_step,
        grad_bc,
        grad_ssm_out,
        grad_gain_two,
        grad_gate,
        grad_up,
        grad_down,
    )
    scattered = (
        lax.psum_scatter(
            weight_grads[0].astype(jnp.bfloat16), "shard", scatter_dimension=0, tiled=True
        ).astype(jnp.float32),
        lax.psum_scatter(
            weight_grads[1].astype(jnp.bfloat16), "shard", scatter_dimension=0, tiled=True
        ).astype(jnp.float32),
        lax.psum_scatter(
            weight_grads[2].astype(jnp.bfloat16), "shard", scatter_dimension=0, tiled=True
        ).astype(jnp.float32),
        lax.psum_scatter(
            weight_grads[3].astype(jnp.bfloat16), "shard", scatter_dimension=1, tiled=True
        ).astype(jnp.float32),
        lax.psum_scatter(
            weight_grads[4].astype(jnp.bfloat16), "shard", scatter_dimension=0, tiled=True
        ).astype(jnp.float32),
        lax.psum_scatter(
            weight_grads[5].astype(jnp.bfloat16), "shard", scatter_dimension=0, tiled=True
        ).astype(jnp.float32),
        lax.psum_scatter(
            weight_grads[6].astype(jnp.bfloat16), "shard", scatter_dimension=0, tiled=True
        ).astype(jnp.float32),
        lax.psum_scatter(
            weight_grads[7].astype(jnp.bfloat16), "shard", scatter_dimension=0, tiled=True
        ).astype(jnp.float32),
        lax.psum_scatter(
            weight_grads[8].astype(jnp.bfloat16), "shard", scatter_dimension=1, tiled=True
        ).astype(jnp.float32),
        lax.psum_scatter(
            weight_grads[9].astype(jnp.bfloat16), "shard", scatter_dimension=0, tiled=True
        ).astype(jnp.float32),
        lax.psum_scatter(
            weight_grads[10].astype(jnp.bfloat16), "shard", scatter_dimension=0, tiled=True
        ).astype(jnp.float32),
        lax.psum_scatter(
            weight_grads[11].astype(jnp.bfloat16), "shard", scatter_dimension=0, tiled=True
        ).astype(jnp.float32),
        lax.psum_scatter(
            weight_grads[12].astype(jnp.bfloat16), "shard", scatter_dimension=1, tiled=True
        ).astype(jnp.float32),
    )
    summed = (
        lax.psum(scattered[0].astype(jnp.bfloat16), "ctx").astype(jnp.float32),
        lax.psum(scattered[1].astype(jnp.bfloat16), "ctx").astype(jnp.float32),
        lax.psum(scattered[2].astype(jnp.bfloat16), "ctx").astype(jnp.float32),
        lax.psum(scattered[3].astype(jnp.bfloat16), "ctx").astype(jnp.float32),
        lax.psum(scattered[4].astype(jnp.bfloat16), "ctx").astype(jnp.float32),
        lax.psum(scattered[5].astype(jnp.bfloat16), "ctx").astype(jnp.float32),
        lax.psum(scattered[6].astype(jnp.bfloat16), "ctx").astype(jnp.float32),
        lax.psum(scattered[7].astype(jnp.bfloat16), "ctx").astype(jnp.float32),
        lax.psum(scattered[8].astype(jnp.bfloat16), "ctx").astype(jnp.float32),
        lax.psum(scattered[9].astype(jnp.bfloat16), "ctx").astype(jnp.float32),
        lax.psum(scattered[10].astype(jnp.bfloat16), "ctx").astype(jnp.float32),
        lax.psum(scattered[11].astype(jnp.bfloat16), "ctx").astype(jnp.float32),
        lax.psum(scattered[12].astype(jnp.bfloat16), "ctx").astype(jnp.float32),
    )
    tp_rank = lax.axis_index("tp")
    tp_count = lax.axis_size("tp")

    def widen(values, along):
        shape = list(values.shape)
        width = shape[along]
        shape[along] = width * tp_count
        return lax.dynamic_update_slice_in_dim(
            jnp.zeros(tuple(shape), jnp.float32), values, tp_rank * width, along
        )

    def narrow(values, along, width):
        return lax.dynamic_slice_in_dim(values, tp_rank * width, width, along)

    head_sums = lax.psum(
        (
            widen(grad_bias, 0),
            widen(grad_decay, 0),
            widen(grad_skip, 0),
            widen(grad_convx_taps, 1),
            widen(grad_convx_bias, 0),
            grad_convbc_taps,
            grad_convbc_bias,
        ),
        ("shard", "ctx", "tp"),
    )
    inner_local = grad_convx_bias.shape[0]
    return (
        result,
        grad_tokens,
        summed[0],
        summed[1],
        summed[2],
        summed[3],
        summed[4],
        summed[5],
        summed[6],
        summed[7],
        narrow(head_sums[3], 1, inner_local),
        narrow(head_sums[4], 0, inner_local),
        head_sums[5],
        head_sums[6],
        narrow(head_sums[0], 0, mamba_local),
        narrow(head_sums[1], 0, mamba_local),
        narrow(head_sums[2], 0, mamba_local),
        summed[8],
        summed[9],
        summed[10],
        summed[11],
        summed[12],
    )


def solution(mesh):
    return jax.shard_map(
        local,
        mesh=mesh,
        in_specs=(
            P(("shard", "ctx"), None),
            P("shard"),
            P("shard"),
            P("shard", "tp"),
            P("shard", "tp"),
            P("tp", "shard"),
            P("shard", "tp"),
            P("shard", "tp"),
            P("shard", "tp"),
            P("shard", None),
            P(None, "tp"),
            P("tp"),
            P(),
            P(),
            P("tp"),
            P("tp"),
            P("tp"),
            P("tp", "shard"),
            P("shard"),
            P("shard", "tp"),
            P("shard", "tp"),
            P("tp", "shard"),
            P(("shard", "ctx"), None),
        ),
        out_specs=(
            P(("shard", "ctx"), None),
            P(("shard", "ctx"), None),
            P("shard"),
            P("shard", "tp"),
            P("shard", "tp"),
            P("tp", "shard"),
            P("shard", "tp"),
            P("shard", "tp"),
            P("shard", "tp"),
            P("shard", None),
            P(None, "tp"),
            P("tp"),
            P(),
            P(),
            P("tp"),
            P("tp"),
            P("tp"),
            P("tp", "shard"),
            P("shard"),
            P("shard", "tp"),
            P("shard", "tp"),
            P("tp", "shard"),
        ),
        check_vma=False,
    )
```

profile of v0, /device:TPU:0, one launch (start us, length us, event | category | flops | bytes accessed | tf_op | source)
XLA Modules:
  0.0 1461.6 jit_solution(6114938702491037060)
XLA Ops:
  32.7 13.8 all_gather.74
  104.9 15.5 %all_gather.68 = bf16[2048,128]{0,1:T(8,128)(2,1)} all-gather(bf16[512,128]{0,1:T(8,128)(2,1)S(1)} %pad_maximum_fusion.3), channel_id=1, replica_groups=mesh['shard'=4,'ctx'=4,'tp'=2] {'ctx'}, dimensions={0}, use_global_device_ids=true | all-gather | bytes 655360 | tf_op jit(solution)/shard_map/all_gather | solution.py:292
  120.7 53.6 %while.143 = (s32[]{:T(128)}, f32[4,512]{1,0:T(4,128)S(1)}, f32[4,512]{1,0:T(4,128)S(1)}, f32[4,512,64]{1,2,0:T(8,128)}, s32[4]{0:T(128)S(1)}, /*index=5*/s32[51...) while((s32[]{:T(128)}, f32[4,512]{1,0:T(4,128)S(1)}, ...), condition=%wide.region_6.7_spmd.clone, body=%wide.region_3.6_spmd.clone.sunk | while | flops 282209280 | bytes 15220983 | solution.py:328
  219.8 202.3 %while.144 = (s32[]{:T(128)}, f32[12,64,128]{2,1,0:T(8,128)S(1)}, s32[]{:T(128)}, f32[4,128,12,64]{1,0,3,2:T(4,128)}, f32[4,128,128,12]{2,1,3,0:T(8,128)}, /*ind...) while((s32[]{:T(128)}, f32[12,64,128]{2,1,0:T(8,128)S(1)}, ...), condition=%wide.region_9.10_spmd.clone, body=%wide.region_7.9_spmd.clone.sunk | while | flops 482043136 | bytes 10746573 | solution.py:168
  422.2 16.4 %all-gather.1 = bf16[48,64,128]{2,1,0:T(8,128)(2,1)} all-gather(bf16[12,64,128]{2,1,0:T(8,128)(2,1)S(1)} %convert_element_type.341), channel_id=3, replica_groups=mesh['shard'=4,'ctx'=4,'tp'=2] {'ctx'}, dimensions={0}, use_global_device_ids=true | all-gather | bytes 983040 | tf_op jit(solution)/shard_map/all_gather | solution.py:22
  464.4 17.7 %all-gather.6 = bf16[4,1,256]{2,1,0:T(2,128)(2,1)S(1)} all-gather(bf16[1,1,256]{2,1,0:T(2,128)(2,1)S(1)} %reshape.956), channel_id=1, replica_groups=mesh['shard'=4,'ctx'=4,'tp'=2] {'shard'}, dimensions={0}, use_global_device_ids=true | all-gather | bytes 2560 | tf_op jit(solution)/shard_map/all_gather | solution.py:230
  489.9 29.4 %all-gather.20.cloned.1.call-done = bf16[1024,1024]{1,0:T(8,128)(2,1)} async-done(((bf16[256,1024]{1,0:T(8,128)(2,1)}), bf16[1024,1024]{1,0:T(8,128)(2,1)}) %all-gather.20.cloned.1.call-update) | async-done | bytes 2097168 | tf_op jit(solution)/shard_map/all_gather | solution.py:231
  523.8 32.8 %all-gather.22.cloned.1.call-done = bf16[1024,1024]{1,0:T(8,128)(2,1)} async-done(((bf16[256,1024]{1,0:T(8,128)(2,1)}), bf16[1024,1024]{1,0:T(8,128)(2,1)}) %all-gather.22.cloned.1.call-update) | async-done | bytes 2097168 | tf_op jit(solution)/shard_map/all_gather | solution.py:232
  605.4 20.2 %all-gather.2 = bf16[48,64,128]{2,1,0:T(8,128)(2,1)} all-gather(bf16[12,64,128]{2,1,0:T(8,128)(2,1)S(1)} %fusion.173), channel_id=4, replica_groups=mesh['shard'=4,'ctx'=4,'tp'=2] {'ctx'}, dimensions={0}, use_global_device_ids=true | all-gather | bytes 983040 | tf_op jit(solution)/shard_map/all_gather | solution.py:47
  639.7 172.5 %while.147 = (s32[]{:T(128)}, f32[12]{0:T(128)}, f32[12,64,128]{2,1,0:T(8,128)S(1)}, f32[4,128,12,64]{1,0,3,2:T(4,128)}, f32[4,128,128]{2,1,0:T(8,128)}, /*index...) while((s32[]{:T(128)}, f32[12]{0:T(128)}, ...), condition=%wide.region_36.37_spmd.clone, body=%wide.region_26.36_spmd.clone.sunk | while | flops 959580160 | bytes 17784852 | solution.py:168
  839.1 60.4 %while.146 = (s32[]{:T(128)}, f32[4,512,64]{1,2,0:T(8,128)S(1)}, bf16[4,512,128]{1,2,0:T(8,128)(2,1)}, s32[4]{0:T(128)S(1)}, s32[512]{0:T(512)}, /*index=5*/s32[...) while((s32[]{:T(128)}, f32[4,512,64]{1,2,0:T(8,128)S(1)}, ...), condition=%wide.region_22.23_spmd.clone, body=%wide.region_21.22_spmd.clone.sunk | while | flops 684131328 | bytes 40215368 | solution.py:463
  903.6 16.2 %all-reduce.26 = (bf16[12,768]{1,0:T(8,128)(2,1)S(1)}, bf16[12,256]{1,0:T(8,128)(2,1)S(1)}) all-reduce(bf16[12,768]{1,0:T(8,128)(2,1)S(1)} %dynamic_update_slice.205, bf16[12,256]{1,0:T(8,128)(2,1)S(1)} %dynamic_update_slice.206), channel_id=6, replica_groups=mesh['shard'=4,'ctx'=4,'tp'=2] {'ctx'}, use_global_device_ids=true, to_apply=%region_37.38.clone | all-reduce | flops 12288 | bytes 49152
  970.1 17.0 %reduce-scatter.19.cloned.1.call-done = bf16[256,256]{1,0:T(8,128)(2,1)} async-done(((bf16[256,1024]{1,0:T(8,128)(2,1)}), bf16[256,256]{1,0:T(8,128)(2,1)}) %reduce-scatter.19.cloned.1.call-update) | async-done | bytes 131088 | tf_op jit(solution)/shard_map/reduce_scatter | solution.py:567
  987.2 27.3 %reduce-scatter.17.cloned.1.call-done = bf16[256,128]{1,0:T(8,128)(2,1)} async-done(((bf16[1024,128]{1,0:T(8,128)(2,1)}), bf16[256,128]{1,0:T(8,128)(2,1)}) %reduce-scatter.17.cloned.1.call-update) | async-done | bytes 65552 | tf_op jit(solution)/shard_map/reduce_scatter | solution.py:564
  1014.5 28.5 %reduce-scatter.15.cloned.1.call-done = bf16[256,256]{1,0:T(8,128)(2,1)} async-done(((bf16[1024,256]{1,0:T(8,128)(2,1)}), bf16[256,256]{1,0:T(8,128)(2,1)}) %reduce-scatter.15.cloned.1.call-update) | async-done | bytes 131088 | tf_op jit(solution)/shard_map/reduce_scatter | solution.py:561
  1042.9 38.0 %reduce-scatter.33.cloned.1.call-done = bf16[256,1024]{1,0:T(8,128)(2,1)} async-done(((bf16[1024,1024]{1,0:T(8,128)(2,1)}), bf16[256,1024]{1,0:T(8,128)(2,1)}) %reduce-scatter.33.cloned.1.call-update) | async-done | bytes 524304 | tf_op jit(solution)/shard_map/reduce_scatter | solution.py:591
  1081.0 38.3 %reduce-scatter.31.cloned.1.call-done = bf16[256,1024]{1,0:T(8,128)(2,1)} async-done(((bf16[1024,1024]{1,0:T(8,128)(2,1)}), bf16[256,1024]{1,0:T(8,128)(2,1)}) %reduce-scatter.31.cloned.1.call-update) | async-done | bytes 524304 | tf_op jit(solution)/shard_map/reduce_scatter | solution.py:588
  1119.3 33.8 %reduce-scatter.29.cloned.1.call-done = bf16[768,256]{1,0:T(8,128)(2,1)} async-done(((bf16[768,1024]{1,0:T(8,128)(2,1)}), bf16[768,256]{1,0:T(8,128)(2,1)}) %reduce-scatter.29.cloned.1.call-update) | async-done | bytes 393232 | tf_op jit(solution)/shard_map/reduce_scatter | solution.py:582
  1153.0 33.8 %reduce-scatter.23.cloned.1.call-done = bf16[256,768]{1,0:T(8,128)(2,1)} async-done(((bf16[1024,768]{1,0:T(8,128)(2,1)}), bf16[256,768]{1,0:T(8,128)(2,1)}) %reduce-scatter.23.cloned.1.call-update) | async-done | bytes 393232 | tf_op jit(solution)/shard_map/reduce_scatter | solution.py:573
  1186.8 33.8 %reduce-scatter.21.cloned.1.call-done = bf16[256,768]{1,0:T(8,128)(2,1)} async-done(((bf16[1024,768]{1,0:T(8,128)(2,1)}), bf16[256,768]{1,0:T(8,128)(2,1)}) %reduce-scatter.21.cloned.1.call-update) | async-done | bytes 393232 | tf_op jit(solution)/shard_map/reduce_scatter | solution.py:570
  1220.7 38.2 %reduce-scatter.35.cloned.1.call-done = bf16[1024,256]{1,0:T(8,128)(2,1)} async-done(((bf16[1024,1024]{1,0:T(8,128)(2,1)}), bf16[1024,256]{1,0:T(8,128)(2,1)}) %reduce-scatter.35.cloned.1.call-update) | async-done | bytes 524304 | tf_op jit(solution)/shard_map/reduce_scatter | solution.py:594
  1258.8 28.3 %reduce-scatter.27.cloned.1.call-done = bf16[256,256]{1,0:T(8,128)(2,1)} async-done(((bf16[1024,256]{1,0:T(8,128)(2,1)}), bf16[256,256]{1,0:T(8,128)(2,1)}) %reduce-scatter.27.cloned.1.call-update) | async-done | bytes 131088 | tf_op jit(solution)/shard_map/reduce_scatter | solution.py:579
  1289.6 40.1 %all-reduce.24 = (f32[4,1536]{1,0:T(4,128)S(1)}, f32[1536]{0:T(1024)S(1)}, f32[4,256]{1,0:T(4,128)}, f32[256]{0:T(256)}, f32[24]{0:T(128)S(1)}, /*index=5*/f32[24]{0:T(128)S(1)}, f32[24]{0:T(128)S(1)}) all-reduce(f32[4,1536]{1,0:T(4,128)S(1)} %add_dynamic-update-slice_fusion, ...), channel_id=1, replica_groups=mesh['shard'=4,'ctx'=4,'tp'=2] {'shard','ctx','tp'}, use_global_device_ids=true, to_apply=%region_67.68 | all-reduce | flops 9032 | bytes 72256 | tf_op jit(solution)/shard_map/psum | solution.py:627
  1365.2 78.3 %all-reduce.39.cloned.1.call-done = (bf16[256,256]{1,0:T(8,128)(2,1)}, bf16[256,128]{1,0:T(8,128)(2,1)}, bf16[256,256]{1,0:T(8,128)(2,1)}, bf16[256,768]{1,0:T(8...) async-done(((bf16[256,256]{1,0:T(8,128)(2,1)}, ...) | async-done | bytes 3211280 | tf_op jit(solution)/shard_map/psum | solution.py:600
  (1090 shorter events, 839.4 us)
Async XLA Ops:
  7.2 181.6 %all-gather.14.cloned.1.call-start = ((), (), s32[]{:S(2)}) async-start(), calls=%async_computation.12 | async-start | bytes 1966080 | tf_op jit(solution)/shard_map/all_gather | solution.py:226
  8.0 446.2 %all-gather.16.cloned.1.call-start = ((), (), s32[]{:S(2)}) async-start(), calls=%async_computation.13 | async-start | bytes 1966080 | tf_op jit(solution)/shard_map/all_gather | solution.py:225
  8.7 450.1 %all-gather.18.cloned.1.call-start = ((), (), s32[]{:S(2)}) async-start(), calls=%async_computation.14 | async-start | bytes 1966080 | tf_op jit(solution)/shard_map/all_gather | solution.py:229
  9.4 472.7 %all-gather.24.cloned.1.call-start = ((), (), s32[]{:S(2)}) async-start(), calls=%async_computation.18 | async-start | bytes 2621440 | tf_op jit(solution)/shard_map/all_gather | solution.py:233
  10.0 476.3 %all-reduce.35.cloned.1.call-start = ((), (), s32[]{:S(2)}) async-start(), calls=%async_computation.15 | async-start | bytes 2097152 | tf_op jit(solution)/shard_map/psum | solution.py:395
  463.0 56.2 %all-gather.20.cloned.1.call-start = ((), (), s32[]{:S(2)}) async-start(), calls=%async_computation.16 | async-start | bytes 2621440 | tf_op jit(solution)/shard_map/all_gather | solution.py:231
  463.6 92.9 %all-gather.22.cloned.1.call-start = ((), (), s32[]{:S(2)}) async-start(), calls=%async_computation.17 | async-start | bytes 2621440 | tf_op jit(solution)/shard_map/all_gather | solution.py:232
  464.4 123.7 %all-reduce.37.cloned.1.call-start = ((), (), s32[]{:S(2)}) async-start(), calls=%async_computation.19 | async-start | bytes 2097152 | tf_op jit(solution)/shard_map/psum | solution.py:414
  568.3 362.4 %reduce-scatter.13.cloned.1.call-start = ((), (), s32[]{:S(2)}) async-start(), calls=%async_computation.20 | async-start | bytes 655360 | tf_op jit(solution)/shard_map/reduce_scatter | solution.py:503
  901.6 65.0 %all-reduce.41.cloned.1.call-start = ((), (), s32[]{:S(2)}) async-start(), calls=%async_computation.33 | async-start | bytes 4718592 | tf_op jit(solution)/shard_map/psum | solution.py:404
  936.8 50.4 %reduce-scatter.19.cloned.1.call-start = ((), (), s32[]{:S(2)}) async-start(), calls=%async_computation.23 | async-start | bytes 655360 | tf_op jit(solution)/shard_map/reduce_scatter | solution.py:567
  939.3 75.2 %reduce-scatter.17.cloned.1.call-start = ((), (), s32[]{:S(2)}) async-start(), calls=%async_computation.22 | async-start | bytes 327680 | tf_op jit(solution)/shard_map/reduce_scatter | solution.py:564
  940.8 102.2 %reduce-scatter.15.cloned.1.call-start = ((), (), s32[]{:S(2)}) async-start(), calls=%async_computation.21 | async-start | bytes 655360 | tf_op jit(solution)/shard_map/reduce_scatter | solution.py:561
  942.3 138.7 %reduce-scatter.33.cloned.1.call-start = ((), (), s32[]{:S(2)}) async-start(), calls=%async_computation.30 | async-start | bytes 2621440 | tf_op jit(solution)/shard_map/reduce_scatter | solution.py:591
  947.4 171.9 %reduce-scatter.31.cloned.1.call-start = ((), (), s32[]{:S(2)}) async-start(), calls=%async_computation.29 | async-start | bytes 2621440 | tf_op jit(solution)/shard_map/reduce_scatter | solution.py:588
  951.9 201.1 %reduce-scatter.29.cloned.1.call-start = ((), (), s32[]{:S(2)}) async-start(), calls=%async_computation.28 | async-start | bytes 1966080 | tf_op jit(solution)/shard_map/reduce_scatter | solution.py:582
  955.3 231.5 %reduce-scatter.23.cloned.1.call-start = ((), (), s32[]{:S(2)}) async-start(), calls=%async_computation.25 | async-start | bytes 1966080 | tf_op jit(solution)/shard_map/reduce_scatter | solution.py:573
  959.0 261.7 %reduce-scatter.21.cloned.1.call-start = ((), (), s32[]{:S(2)}) async-start(), calls=%async_computation.24 | async-start | bytes 1966080 | tf_op jit(solution)/shard_map/reduce_scatter | solution.py:570
  962.5 296.3 %reduce-scatter.35.cloned.1.call-start = ((), (), s32[]{:S(2)}) async-start(), calls=%async_computation.31 | async-start | bytes 2621440 | tf_op jit(solution)/shard_map/reduce_scatter | solution.py:594
  966.5 320.7 %reduce-scatter.27.cloned.1.call-start = ((), (), s32[]{:S(2)}) async-start(), calls=%async_computation.27 | async-start | bytes 655360 | tf_op jit(solution)/shard_map/reduce_scatter | solution.py:579
  969.0 377.9 %reduce-scatter.25.cloned.1.call-start = ((), (), s32[]{:S(2)}) async-start(), calls=%async_computation.26 | async-start | bytes 40960 | tf_op jit(solution)/shard_map/reduce_scatter | solution.py:576
  970.1 362.6 %copy-start.62 = (bf16[1024,256]{1,0:T(8,128)(2,1)S(1)}, bf16[1024,256]{1,0:T(8,128)(2,1)}, u32[]{:S(2)}) copy-start(bf16[1024,256]{1,0:T(8,128)(2,1)} %copy-done.61) | copy-start | bytes 1572868
  970.1 362.6 %copy-start.165 = (bf16[512,256]{1,0:T(8,128)(2,1)S(1)}, bf16[512,256]{1,0:T(8,128)(2,1)}, u32[]{:S(2)}) copy-start(bf16[512,256]{1,0:T(8,128)(2,1)} %get-tuple-element.2214) | copy-start | bytes 786436
  970.1 473.4 %all-reduce.39.cloned.1.call-start = ((), (), s32[]{:S(2)}) async-start(), calls=%async_computation.32 | async-start | bytes 6422528 | tf_op jit(solution)/shard_map/psum | solution.py:600
  (206 other events, 3321.4 us)
Sparse Core Ops, SparseCore 0:
  9.9 38.5 all-gather.13
  50.4 31.2 all-gather.15
  83.4 31.9 all-gather.17
  117.1 35.1 all-gather.23
  463.2 17.6 all-reduce.34
  482.7 36.4 all-gather.19
  521.2 35.2 all-gather.21
  568.4 19.5 all-reduce.36
  901.7 20.0 reduce-scatter.12
  936.9 21.1 all-reduce.40
  961.2 25.9 reduce-scatter.18
  990.4 24.0 reduce-scatter.16
  1018.1 24.7 reduce-scatter.14
  1045.8 35.1 reduce-scatter.32
  1084.0 35.1 reduce-scatter.30
  1122.1 30.8 reduce-scatter.28
  1155.9 30.9 reduce-scatter.22
  1189.7 30.9 reduce-scatter.20
  1223.6 35.1 reduce-scatter.34
  1262.3 24.7 reduce-scatter.26
  1290.4 22.4 reduce-scatter.24
  1316.1 127.2 all-reduce.38
where the time goes:
time: 1480 us; the launch traced here: 1460 us
  waiting for transfers between devices  475 us (32%)
  matrix products  282 us (19%)
  local copies, waits for them, and re-layouts  249 us (17%)
  blocking collectives  249 us (17%)
  other arithmetic  172 us (12%)
  between operations  20.3 us (1%)
    dynamic_update_slice x60, local copies, waits for them, and re-layouts, ssm_local(): lax.scan(partial(span_step, decay_rates), initial, (to_blocks(inputs), to...  129 us
    psum x1, waiting for transfers between devices, local(): lax.psum(scattered[1].astype(jnp.bfloat16), 'ctx').astype(jnp.float32)  78.3 us
    psum x1, blocking collectives, local(): lax.psum((widen(grad_bias, 0), widen(grad_decay, 0), widen(grad_skip, 0),...  40.1 us
    dot_general x12, matrix products, span_step(): outputs = jnp.einsum('tuh,uhp->thp', weighted, inflow, precision=HIGHEST)  39 us
    reduce_scatter x1, waiting for transfers between devices, local(): lax.psum_scatter(weight_grads[10].astype(jnp.bfloat16), 'shard', scatter_...  38.3 us
    reduce_scatter x1, waiting for transfers between devices, local(): lax.psum_scatter(weight_grads[12].astype(jnp.bfloat16), 'shard', scatter_...  38.2 us
    reduce_scatter x1, waiting for transfers between devices, local(): lax.psum_scatter(weight_grads[11].astype(jnp.bfloat16), 'shard', scatter_...  38 us
    unnamed x3, blocking collectives  37.1 us
  transfers between devices with their start and end apart: 22, of which 14 were waited for; matrix products, arithmetic and copies ran while one was open for 26% of the time, Pallas kernels for 0%

commit v1 on v0

v1 whole, which is shorter than its diff:
```python
from functools import partial

import jax
import jax.numpy as jnp
from jax import lax
from jax.experimental import pallas as pl
from jax.experimental.pallas import tpu as pltpu
from jax.sharding import PartitionSpec as P

HEAD_SIZE = 64
MP = 64
NS = 128
SPAN = 128
TAPS = 4
QUERY_ROWS = 64
VMEM_BYTES = 48 * 1024 * 1024


HIGHEST = lax.Precision.HIGHEST
ROPE_BASE = 100000000000.0


def rms_scale(values):
    return lax.rsqrt(jnp.mean(values * values, axis=-1, keepdims=True) + 1e-05)


def norm_back(values, scale, gain, d_normed):
    scaled = d_normed * gain[None, :]
    d_values = scale * scaled - values * scale**3 * jnp.mean(
        scaled * values, axis=-1, keepdims=True
    )
    return (d_values, jnp.sum(d_normed * values * scale, axis=0))


def contract_rows(former, latter):
    return lax.dot_general(
        former, latter, (((0,), (0,)), ((), ())), preferred_element_type=jnp.float32
    )


def contract_cols(former, latter):
    return lax.dot_general(
        former, latter, (((1,), (1,)), ((), ())), preferred_element_type=jnp.float32
    )


def silu_slope(values):
    sigma = jax.nn.sigmoid(values)
    return sigma * (1.0 + values * (1.0 - sigma))


def positions_in_group(segments):
    count = segments.shape[0]
    index = jnp.arange(count, dtype=jnp.int32)
    fresh = jnp.concatenate([jnp.ones((1,), bool), segments[1:] != segments[:-1]])
    starts = lax.cummax(jnp.where(fresh, index, 0), axis=0)
    return index - starts


def conv_silu(extended, taps, bias, seg_ext):
    reach = taps.shape[0] - 1
    packed_length = extended.shape[0] - reach
    current = seg_ext[reach:]
    total = jnp.zeros((packed_length, extended.shape[1]), jnp.float32) + bias[None, :]
    for delay in range(taps.shape[0]):
        source = extended[reach - delay : reach - delay + packed_length]
        same = (seg_ext[reach - delay : reach - delay + packed_length] == current)[:, None]
        total = total + jnp.where(same, taps[delay][None, :] * source, 0.0)
    return jax.nn.silu(total)


def dot_nn(a, b):
    return lax.dot_general(a, b, (((1,), (0,)), ((), ())), preferred_element_type=jnp.float32)


def rope_tables(positions, width):
    lane = jnp.arange(width, dtype=jnp.int32) % (HEAD_SIZE // 2)
    frequency = ROPE_BASE ** (-(2.0 * lane.astype(jnp.float32)) / HEAD_SIZE)
    angle = positions.astype(jnp.float32)[:, None] * frequency[None, :]
    return (jnp.cos(angle), jnp.sin(angle))


def rotate(values, cosine, sine):
    half = HEAD_SIZE // 2
    lane = lax.broadcasted_iota(jnp.int32, values.shape, 1) % HEAD_SIZE
    turned = jnp.where(lane < half, -jnp.roll(values, -half, 1), jnp.roll(values, half, 1))
    return values * cosine + turned * sine


def tp_sum(values):
    low = values.astype(jnp.bfloat16)
    other = lax.ppermute(low, "tp", [(0, 1), (1, 0)])
    return low.astype(jnp.float32) + other.astype(jnp.float32)


def stack_heads(block, heads):
    return jnp.concatenate(
        [block[:, h * HEAD_SIZE : (h + 1) * HEAD_SIZE] for h in range(heads)], axis=0
    )


def masked_scores(q, keys, low_ref, high_ref, heads):
    scores = contract_cols(q, keys) * (HEAD_SIZE**-0.5)
    place = lax.broadcasted_iota(jnp.int32, scores.shape, 1)
    low = jnp.concatenate([low_ref[...]] * heads, axis=0)
    high = jnp.concatenate([high_ref[...]] * heads, axis=0)
    return jnp.where((place >= low) & (place <= high), scores, -1e30)


def attn_fwd_kernel(heads, q_ref, kv_ref, low_ref, high_ref, out_ref, lse_ref):
    rows = q_ref.shape[0]
    q = stack_heads(q_ref[...], heads)
    scores = masked_scores(q, kv_ref[:, :HEAD_SIZE], low_ref, high_ref, heads)
    top = jnp.max(scores, axis=1, keepdims=True)
    expon = jnp.exp(scores - top)
    total = jnp.sum(expon, axis=1, keepdims=True)
    out = dot_nn(expon.astype(jnp.bfloat16), kv_ref[:, HEAD_SIZE:]) / total
    for h in range(heads):
        out_ref[:, h * HEAD_SIZE : (h + 1) * HEAD_SIZE] = out[h * rows : (h + 1) * rows]
    lse_ref[...] = top + jnp.log(total)


def attn_bwd_kernel(
    heads, q_ref, kv_ref, low_ref, high_ref, out_ref, lse_ref, do_ref, dq_ref, dkv_ref
):
    rows = q_ref.shape[0]
    scaling = HEAD_SIZE**-0.5

    @pl.when(pl.program_id(0) == 0)
    def _():
        dkv_ref[...] = jnp.zeros_like(dkv_ref)

    q = stack_heads(q_ref[...], heads)
    d_out = stack_heads(do_ref[...], heads)
    delta = jnp.sum(
        d_out.astype(jnp.float32) * stack_heads(out_ref[...], heads), axis=1, keepdims=True
    )
    keys = kv_ref[:, :HEAD_SIZE]
    scores = masked_scores(q, keys, low_ref, high_ref, heads)
    probs = jnp.exp(scores - lse_ref[...])
    d_probs = contract_cols(d_out, kv_ref[:, HEAD_SIZE:])
    d_scores = (probs * (d_probs - delta)).astype(jnp.bfloat16)
    dq = dot_nn(d_scores, keys) * scaling
    for h in range(heads):
        dq_ref[:, h * HEAD_SIZE : (h + 1) * HEAD_SIZE] = dq[h * rows : (h + 1) * rows]
    dkv_ref[:, :HEAD_SIZE] += contract_rows(d_scores, q) * scaling
    dkv_ref[:, HEAD_SIZE:] += contract_rows(probs.astype(jnp.bfloat16), d_out)


def attn_specs(width, keys, heads):
    rows = pl.BlockSpec((QUERY_ROWS, width), lambda i: (i, 0))
    group = pl.BlockSpec((keys, 2 * HEAD_SIZE), lambda i: (0, 0))
    column = pl.BlockSpec((QUERY_ROWS, 1), lambda i: (i, 0))
    stacked = pl.BlockSpec((QUERY_ROWS * heads, 1), lambda i: (i, 0))
    return (rows, group, column, stacked)


def attn_forward(queries, kv, low, high):
    count, width = queries.shape
    heads = width // HEAD_SIZE
    rows, group, column, stacked = attn_specs(width, kv.shape[0], heads)
    return pl.pallas_call(
        partial(attn_fwd_kernel, heads),
        grid=(count // QUERY_ROWS,),
        in_specs=[rows, group, column, column],
        out_specs=[rows, stacked],
        out_shape=[
            jax.ShapeDtypeStruct((count, width), jnp.float32),
            jax.ShapeDtypeStruct((count * heads, 1), jnp.float32),
        ],
        compiler_params=pltpu.CompilerParams(vmem_limit_bytes=VMEM_BYTES),
        cost_estimate=pl.CostEstimate(
            flops=4 * count * kv.shape[0] * width,
            bytes_accessed=4 * count * width,
            transcendentals=count * heads * kv.shape[0],
        ),
        name="attn_forward",
    )(queries, kv, low, high)


def attn_backward(queries, kv, low, high, out, lse, d_out):
    count, width = queries.shape
    heads = width // HEAD_SIZE
    rows, group, column, stacked = attn_specs(width, kv.shape[0], heads)
    return pl.pallas_call(
        partial(attn_bwd_kernel, heads),
        grid=(count // QUERY_ROWS,),
        in_specs=[rows, group, column, column, rows, stacked, rows],
        out_specs=[rows, group],
        out_shape=[
            jax.ShapeDtypeStruct((count, width), jnp.float32),
            jax.ShapeDtypeStruct(kv.shape, jnp.float32),
        ],
        compiler_params=pltpu.CompilerParams(vmem_limit_bytes=VMEM_BYTES),
        cost_estimate=pl.CostEstimate(
            flops=10 * count * kv.shape[0] * width,
            bytes_accessed=8 * count * width,
            transcendentals=count * heads * kv.shape[0],
        ),
        name="attn_backward",
    )(queries, kv, low, high, out, lse, d_out)


def pair_lanes(columns, pair, shape):
    lane = lax.broadcasted_iota(jnp.int32, shape, 1)
    return jnp.where(
        lane < MP, columns[:, 2 * pair : 2 * pair + 1], columns[:, 2 * pair + 1 : 2 * pair + 2]
    )


def split_pair(values):
    lane = lax.broadcasted_iota(jnp.int32, values.shape, 1)
    zero = jnp.zeros_like(values)
    return jnp.concatenate(
        [jnp.where(lane < MP, values, zero), jnp.where(lane < MP, zero, values)], axis=0
    )


def span_mask(segc_ref, segr_ref):
    row = lax.broadcasted_iota(jnp.int32, (SPAN, SPAN), 0)
    col = lax.broadcasted_iota(jnp.int32, (SPAN, SPAN), 1)
    return (row >= col) & (segc_ref[...] == segr_ref[...])


def head_decay(mask, cum, cum_t_ref, head):
    spread = cum[:, head : head + 1] - cum_t_ref[head : head + 1, :]
    return jnp.where(mask, jnp.exp(jnp.minimum(spread, 0.0)), 0.0)


def pair_keep(entry, pair):
    row = lax.broadcasted_iota(jnp.int32, (2 * MP, NS), 0)
    last = entry[SPAN - 1 : SPAN, :]
    return jnp.where(
        row < MP, last[:, 2 * pair : 2 * pair + 1], last[:, 2 * pair + 1 : 2 * pair + 2]
    )


def outer_kernel(pairs, v_ref, w_ref, m_ref, out_ref):
    weights = w_ref[...]
    other = m_ref[...]
    for pair in range(pairs):
        block = v_ref[:, pair * 2 * MP : (pair + 1) * 2 * MP]
        block = (block * pair_lanes(weights, pair, block.shape)).astype(jnp.bfloat16)
        out_ref[pair * 2 * MP : (pair + 1) * 2 * MP, :] = contract_rows(block, other)


def weighted_outer(values, weights, other):
    return pl.pallas_call(
        partial(outer_kernel, values.shape[1] // (2 * MP)),
        out_shape=jax.ShapeDtypeStruct((values.shape[1], other.shape[1]), jnp.float32),
        compiler_params=pltpu.CompilerParams(vmem_limit_bytes=VMEM_BYTES),
        name="weighted_outer",
    )(values, weights, other)


def ssm_fwd_kernel(
    pairs,
    x_ref, b_ref, c_ref, step_ref, cum_ref, cum_t_ref, entry_ref, ending_ref, segc_ref, segr_ref,
    init_ref, y_ref, start_ref, state_ref,
):
    @pl.when(pl.program_id(0) == 0)
    def _():
        state_ref[...] = init_ref[...]

    start_ref[0] = state_ref[...]
    b_part, c_part = b_ref[...], c_ref[...]
    steps, cum, entry, ending = step_ref[...], cum_ref[...], entry_ref[...], ending_ref[...]
    mask = span_mask(segc_ref, segr_ref)
    meet = contract_cols(c_part, b_part)
    for pair in range(pairs):
        lanes = slice(pair * 2 * MP, (pair + 1) * 2 * MP)
        shape = (SPAN, 2 * MP)
        inflow = x_ref[:, lanes] * pair_lanes(steps, pair, shape)
        weights = jnp.concatenate(
            [meet * head_decay(mask, cum, cum_t_ref, 2 * pair + k) for k in range(2)], axis=1
        ).astype(jnp.bfloat16)
        state = state_ref[lanes, :]
        y_ref[:, lanes] = dot_nn(weights, split_pair(inflow.astype(jnp.bfloat16))) + pair_lanes(
            entry, pair, shape
        ) * contract_cols(c_part, state.astype(jnp.bfloat16))
        late = (inflow * pair_lanes(ending, pair, shape)).astype(jnp.bfloat16)
        state_ref[lanes, :] = pair_keep(entry, pair) * state + contract_rows(late, b_part)


def ssm_bwd_kernel(
    pairs,
    x_ref, b_ref, c_ref, step_ref, cum_ref, cum_t_ref, entry_ref, ending_ref, segc_ref, segr_ref,
    init_ref, y_ref, start_ref, dy_ref, skip_ref,
    dx_ref, db_ref, dc_ref, dcum_ref, dstep_ref, state_ref,
):
    @pl.when(pl.program_id(0) == 0)
    def _():
        state_ref[...] = init_ref[...]

    b_part, c_part = b_ref[...], c_ref[...]
    steps, cum, entry, ending = step_ref[...], cum_ref[...], entry_ref[...], ending_ref[...]
    mask = span_mask(segc_ref, segr_ref)
    meet = contract_cols(c_part, b_part)
    d_meet = jnp.zeros((SPAN, SPAN), jnp.float32)
    d_b = jnp.zeros((SPAN, NS), jnp.float32)
    d_c = jnp.zeros((SPAN, NS), jnp.float32)
    lane = lax.broadcasted_iota(jnp.int32, (SPAN, 2 * MP), 1)
    token = lax.broadcasted_iota(jnp.int32, (SPAN, 1), 0)
    for pair in range(pairs):
        lanes = slice(pair * 2 * MP, (pair + 1) * 2 * MP)
        shape = (SPAN, 2 * MP)
        x = x_ref[:, lanes]
        step_lanes = pair_lanes(steps, pair, shape)
        end_lanes = pair_lanes(ending, pair, shape)
        inflow = x * step_lanes
        inflow_low = inflow.astype(jnp.bfloat16)
        dy = dy_ref[:, lanes]
        dy_low = dy.astype(jnp.bfloat16)
        dy_split = split_pair(dy_low)
        decays = jnp.concatenate(
            [head_decay(mask, cum, cum_t_ref, 2 * pair + k) for k in range(2)], axis=0
        )
        weights = (jnp.concatenate([meet, meet], axis=0) * decays).astype(jnp.bfloat16)
        grown = contract_cols(dy_split, inflow_low) * decays
        d_meet = d_meet + grown[:SPAN] + grown[SPAN:]
        d_state = state_ref[lanes, :]
        d_state_low = d_state.astype(jnp.bfloat16)
        start = start_ref[0, lanes, :]
        from_end = end_lanes * contract_cols(b_part, d_state_low)
        d_inflow = contract_rows(weights, dy_split) + from_end
        late = (inflow * end_lanes).astype(jnp.bfloat16)
        d_b = d_b + dot_nn(late, d_state_low)
        early = (dy * pair_lanes(entry, pair, shape)).astype(jnp.bfloat16)
        d_c = d_c + dot_nn(early, start.astype(jnp.bfloat16))
        keep = pair_keep(entry, pair)
        kept = keep * d_state * start
        state_ref[lanes, :] = keep * d_state + contract_rows(early, c_part)
        inflow_wide = inflow_low.astype(jnp.float32)
        balance = dy_low.astype(jnp.float32) * y_ref[:, lanes] - inflow_wide * d_inflow
        ended = inflow_wide * from_end
        direct = x * d_inflow
        for k in range(2):
            own = (lane < MP) if k == 0 else (lane >= MP)
            head = 2 * pair + k
            total = jnp.sum(
                jnp.sum(jnp.where(own, ended, 0.0), axis=1, keepdims=True), axis=0, keepdims=True
            ) + jnp.sum(
                jnp.sum(kept[k * MP : (k + 1) * MP], axis=1, keepdims=True), axis=0, keepdims=True
            )
            column = jnp.sum(jnp.where(own, balance, 0.0), axis=1, keepdims=True)
            dcum_ref[:, head : head + 1] = column + jnp.where(token == SPAN - 1, total, 0.0)
            dstep_ref[:, head : head + 1] = jnp.sum(
                jnp.where(own, direct, 0.0), axis=1, keepdims=True
            )
        dx_ref[:, lanes] = step_lanes * d_inflow + skip_ref[:, lanes] * dy
    d_meet_low = d_meet.astype(jnp.bfloat16)
    dc_ref[...] = d_c + dot_nn(d_meet_low, b_part)
    db_ref[...] = d_b + contract_rows(d_meet_low, c_part)


def ssm_specs(count, inner, heads, backward):
    spans = count // SPAN

    def at(i):
        return spans - 1 - i if backward else i

    wide = pl.BlockSpec((SPAN, inner), lambda i: (at(i), 0))
    narrow = pl.BlockSpec((SPAN, NS), lambda i: (at(i), 0))
    per_head = pl.BlockSpec((SPAN, heads), lambda i: (at(i), 0))
    turned = pl.BlockSpec((heads, SPAN), lambda i: (0, at(i)))
    seg_col = pl.BlockSpec((SPAN, 1), lambda i: (at(i), 0))
    seg_row = pl.BlockSpec((1, SPAN), lambda i: (0, at(i)))
    whole = pl.BlockSpec((inner, NS), lambda i: (0, 0))
    starts = pl.BlockSpec((1, inner, NS), lambda i: (at(i), 0, 0))
    flat = pl.BlockSpec((1, inner), lambda i: (0, 0))
    inputs = [wide, narrow, narrow, per_head, per_head, turned, per_head, per_head]
    inputs += [seg_col, seg_row, whole]
    return inputs, wide, narrow, per_head, starts, flat


def ssm_forward(operands, state_in):
    count, inner = operands[0].shape
    heads = operands[3].shape[1]
    inputs, wide, narrow, per_head, starts, flat = ssm_specs(count, inner, heads, False)
    return pl.pallas_call(
        partial(ssm_fwd_kernel, heads // 2),
        grid=(count // SPAN,),
        in_specs=inputs,
        out_specs=[wide, starts],
        out_shape=[
            jax.ShapeDtypeStruct((count, inner), jnp.float32),
            jax.ShapeDtypeStruct((count // SPAN, inner, NS), jnp.float32),
        ],
        scratch_shapes=[pltpu.VMEM((inner, NS), jnp.float32)],
        compiler_params=pltpu.CompilerParams(vmem_limit_bytes=VMEM_BYTES),
        name="ssm_forward",
    )(*operands, state_in)


def ssm_backward(operands, state_grad, y, starting, dy, skip):
    count, inner = operands[0].shape
    heads = operands[3].shape[1]
    inputs, wide, narrow, per_head, starts, flat = ssm_specs(count, inner, heads, True)
    return pl.pallas_call(
        partial(ssm_bwd_kernel, heads // 2),
        grid=(count // SPAN,),
        in_specs=inputs + [wide, starts, wide, flat],
        out_specs=[wide, narrow, narrow, per_head, per_head],
        out_shape=[
            jax.ShapeDtypeStruct((count, inner), jnp.float32),
            jax.ShapeDtypeStruct((count, NS), jnp.float32),
            jax.ShapeDtypeStruct((count, NS), jnp.float32),
            jax.ShapeDtypeStruct((count, heads), jnp.float32),
            jax.ShapeDtypeStruct((count, heads), jnp.float32),
        ],
        scratch_shapes=[pltpu.VMEM((inner, NS), jnp.float32)],
        compiler_params=pltpu.CompilerParams(vmem_limit_bytes=VMEM_BYTES),
        name="ssm_backward",
    )(*operands, state_grad, y, starting, dy, skip)


def span_cumulative(values):
    count, heads = values.shape
    index = jnp.arange(SPAN)
    lower = (index[:, None] >= index[None, :]).astype(jnp.float32)
    spans = values.reshape(count // SPAN, SPAN, heads)
    return jnp.einsum("tu,cuh->cth", lower, spans, precision=HIGHEST).reshape(count, heads)


def span_reverse_cumulative(values):
    count, heads = values.shape
    index = jnp.arange(SPAN)
    upper = (index[:, None] <= index[None, :]).astype(jnp.float32)
    spans = values.reshape(count // SPAN, SPAN, heads)
    return jnp.einsum("tu,cuh->cth", upper, spans, precision=HIGHEST).reshape(count, heads)


def decay_tables(steps, decay_log, seg_local, seg_before):
    count, heads = steps.shape
    spans = count // SPAN
    cum = span_cumulative(steps * (-jnp.exp(decay_log))[None, :])
    by_span = cum.reshape(spans, SPAN, heads)
    seg_spans = seg_local.reshape(spans, SPAN)
    seg_last = seg_spans[:, -1]
    seg_prev = jnp.concatenate([seg_before[None], seg_last[:-1]])
    totals = by_span[:, -1]
    entry = jnp.where((seg_spans == seg_prev[:, None])[..., None], jnp.exp(by_span), 0.0)
    ending = jnp.where(
        (seg_spans == seg_last[:, None])[..., None], jnp.exp(totals[:, None] - by_span), 0.0
    )
    sums = [jnp.zeros_like(totals[0])]
    for span in range(spans):
        sums.append(sums[-1] + totals[span])
    whole = (jnp.stack(sums[:-1])[:, None] + by_span).reshape(count, heads)
    grand = sums[-1]
    seg_end = seg_local[-1]
    entry_all = jnp.where((seg_local == seg_before)[:, None], jnp.exp(whole), 0.0)
    ending_all = jnp.where((seg_local == seg_end)[:, None], jnp.exp(grand[None] - whole), 0.0)
    through = jnp.where(seg_end == seg_before, jnp.exp(grand), 0.0)
    return (
        cum,
        entry.reshape(count, heads),
        ending.reshape(count, heads),
        entry_all,
        ending_all,
        through,
    )


def join_states(states, through, forward):
    length, place = (lax.axis_size("ctx"), lax.axis_index("ctx"))
    order = range(length - 1, -1, -1) if forward else range(length)
    factor = jnp.ones_like(through[0])
    total = jnp.zeros(states.shape[1:], jnp.float32)
    for k in order:
        reached = (k < place) if forward else (k > place)
        weight = jnp.repeat(jnp.where(reached, factor, 0.0), MP)
        total = total + weight[:, None] * states[k].astype(jnp.float32)
        factor = jnp.where(reached, factor * through[k], factor)
    return total


def local(
    tokens, segment, gain_attn, w_query, key_value_weight, w_attn_out, w_gate_z, w_ssm_in, w_step,
    w_bc, w_conv_x, conv_x_bias, w_conv_bc, conv_bc_bias, step_bias, decay_log, skip_gain,
    w_ssm_out, gain_ffn, w_gate, w_up, w_down, grad_out,
):
    qn, kn = w_query.shape[1], key_value_weight.shape[1]
    zn, xn, bn, sn = w_gate_z.shape[1], w_ssm_in.shape[1], w_bc.shape[1], w_step.shape[1]
    fn = w_gate.shape[1]
    an = w_attn_out.shape[0]
    q0, k0, z0, x0 = 0, qn, qn + kn, qn + kn + zn
    b0 = x0 + xn
    s0 = b0 + bn
    g0 = s0 + sn
    first_pack = jnp.concatenate(
        [w_query, key_value_weight, w_gate_z, w_ssm_in, w_bc, w_step]
        + [gain_attn[:, None], gain_ffn[:, None]],
        axis=1,
    )
    out_pack = jnp.concatenate([w_attn_out, w_ssm_out], axis=0).T
    ffn_pack = jnp.concatenate([w_gate, w_up], axis=1)
    full_first = lax.all_gather(first_pack, "shard", axis=0, tiled=True)
    full_out = lax.all_gather(out_pack, "shard", axis=0, tiled=True)
    full_ffn = lax.all_gather(ffn_pack, "shard", axis=0, tiled=True)
    full_down = lax.all_gather(w_down.T, "shard", axis=0, tiled=True)

    row_count = tokens.shape[0]
    ctx_rank = lax.axis_index("ctx")
    ctx_count = lax.axis_size("ctx")
    first_row = ctx_rank * row_count
    seg_local = lax.dynamic_slice_in_dim(segment, first_row, row_count)
    seg_before = jnp.where(
        ctx_rank > 0, lax.dynamic_slice_in_dim(segment, jnp.maximum(first_row - 1, 0), 1)[0], -1
    )
    reach = TAPS - 1
    positions = lax.dynamic_slice_in_dim(positions_in_group(segment), first_row, row_count)
    cos_q, sin_q = rope_tables(positions, qn)
    cosine, sine = cos_q[:, :HEAD_SIZE], sin_q[:, :HEAD_SIZE]
    high = (first_row + jnp.arange(row_count, dtype=jnp.int32))[:, None]
    low = high - positions[:, None]
    seg_padded = jnp.concatenate([jnp.full((reach,), -1, jnp.int32), segment])
    seg_ext = lax.dynamic_slice_in_dim(seg_padded, first_row, row_count + reach)
    hidden_in = tokens.astype(jnp.float32)
    gains = full_first[:, g0:].astype(jnp.float32).T
    gain_one, gain_two = gains[0], gains[1]
    scale_one = rms_scale(hidden_in)
    normalized_input = (hidden_in * scale_one * gain_one[None, :]).astype(jnp.bfloat16)
    proj = jnp.dot(normalized_input, full_first, preferred_element_type=jnp.float32)
    queries = rotate(proj[:, q0:k0], cos_q, sin_q).astype(jnp.bfloat16)
    keyval_raw = proj[:, k0:z0]
    keyval = jnp.concatenate(
        [rotate(keyval_raw[:, :HEAD_SIZE], cosine, sine), keyval_raw[:, HEAD_SIZE:]], axis=-1
    ).astype(jnp.bfloat16)
    raw_x = proj[:, x0:b0].astype(jnp.bfloat16)
    raw_bc = proj[:, b0:s0].astype(jnp.bfloat16)
    gate_z = proj[:, z0:x0]
    step_raw = proj[:, s0:g0]
    onward = [(k, k + 1) for k in range(ctx_count - 1)]
    backward = [(k + 1, k) for k in range(ctx_count - 1)]
    tails = lax.ppermute(
        jnp.concatenate([raw_x[row_count - reach :], raw_bc[row_count - reach :]], axis=1),
        "ctx",
        onward,
    )
    all_keys = lax.all_gather(keyval, "ctx", axis=0, tiled=True)

    ext_x = jnp.concatenate([tails[:, :xn], raw_x], axis=0).astype(jnp.float32)
    ext_bc = jnp.concatenate([tails[:, xn:], raw_bc], axis=0).astype(jnp.float32)
    conv_x, conv_x_back = jax.vjp(
        lambda extended, taps, bias: conv_silu(extended, taps, bias, seg_ext),
        ext_x,
        w_conv_x,
        conv_x_bias,
    )
    conv_bc, conv_bc_back = jax.vjp(
        lambda extended, taps, bias: conv_silu(extended, taps, bias, seg_ext),
        ext_bc,
        w_conv_bc,
        conv_bc_bias,
    )
    steps = jax.nn.softplus(step_raw + step_bias[None, :])
    mamba_local = step_bias.shape[0]
    b_low = conv_bc[:, :NS].astype(jnp.bfloat16)
    c_low = conv_bc[:, NS:].astype(jnp.bfloat16)
    cum, entry, ending, entry_all, ending_all, through = decay_tables(
        steps, decay_log, seg_local, seg_before
    )
    local_state = weighted_outer(conv_x, steps * ending_all, b_low)
    through_row = jnp.zeros((16, NS), jnp.float32).at[0, :mamba_local].set(through)
    state_parts = lax.all_gather(
        jnp.concatenate([local_state, through_row], axis=0).astype(jnp.bfloat16), "ctx"
    )
    attn_out, lse = attn_forward(queries, all_keys, low, high)
    attended = attn_out.astype(jnp.bfloat16)
    all_through = state_parts[:, xn, :mamba_local].astype(jnp.float32)
    state_in = join_states(state_parts[:, :xn], all_through, True)
    operands = (
        conv_x, b_low, c_low, steps, cum, cum.T, entry, ending, seg_local[:, None],
        seg_local[None, :],
    )
    skip_row = jnp.repeat(skip_gain, MP)[None, :]
    y_scan, starting = ssm_forward(operands, state_in)
    scanned = y_scan + skip_row * conv_x
    silu_gate = jax.nn.silu(gate_z)
    gated = (scanned * silu_gate).astype(jnp.bfloat16)
    mixer = jnp.concatenate([attended, gated], axis=1)
    middle = hidden_in + tp_sum(contract_cols(mixer, full_out))

    scale_two = rms_scale(middle)
    normed_ffn = (middle * scale_two * gain_two[None, :]).astype(jnp.bfloat16)
    gate_up = jnp.dot(normed_ffn, full_ffn, preferred_element_type=jnp.float32)
    gate_value, up_value = gate_up[:, :fn], gate_up[:, fn:]
    active = (jax.nn.silu(gate_value) * up_value).astype(jnp.bfloat16)
    d_active = (
        jnp.dot(grad_out, full_down, preferred_element_type=jnp.float32)
        .astype(jnp.bfloat16)
        .astype(jnp.float32)
    )
    d_gate_up = jnp.concatenate(
        [
            (d_active * up_value * silu_slope(gate_value)).astype(jnp.bfloat16),
            (d_active * jax.nn.silu(gate_value)).astype(jnp.bfloat16),
        ],
        axis=1,
    )
    d_normed_ffn = tp_sum(contract_cols(d_gate_up, full_ffn))
    down_part = contract_cols(active, full_down)
    result = (middle + tp_sum(down_part)).astype(jnp.bfloat16)
    grad_down_t = contract_rows(grad_out, active)
    grad_ffn = contract_rows(normed_ffn, d_gate_up)

    def scatter(values):
        part = lax.psum_scatter(
            values.astype(jnp.bfloat16), "shard", scatter_dimension=0, tiled=True
        )
        return lax.psum(part, "ctx").astype(jnp.float32)

    sum_ffn = scatter(jnp.concatenate([grad_ffn, grad_down_t], axis=1))

    d_from_ffn, grad_gain_two = norm_back(middle, scale_two, gain_two, d_normed_ffn)
    d_middle = grad_out.astype(jnp.float32) + d_from_ffn
    d_mid_low = d_middle.astype(jnp.bfloat16)
    d_mixer = jnp.dot(d_mid_low, full_out, preferred_element_type=jnp.float32).astype(jnp.bfloat16)
    d_attended = d_mixer[:, :an]
    d_gated = d_mixer[:, an:].astype(jnp.float32)
    d_scanned = d_gated * silu_gate
    d_gate_z = (d_gated * scanned * silu_slope(gate_z)).astype(jnp.bfloat16)
    grad_skip = jnp.sum((d_scanned * conv_x).reshape(row_count, mamba_local, MP), axis=(0, 2))
    d_state_local = weighted_outer(d_scanned, entry_all, c_low)
    d_state_parts = lax.all_gather(d_state_local.astype(jnp.bfloat16), "ctx")
    d_query, d_kv_group = attn_backward(queries, all_keys, low, high, attn_out, lse, d_attended)
    d_kv_back = lax.psum_scatter(
        d_kv_group.astype(jnp.bfloat16), "ctx", scatter_dimension=0, tiled=True
    ).astype(jnp.float32)
    sum_out = scatter(contract_rows(d_mid_low, mixer))
    state_grad = join_states(d_state_parts, all_through, False)
    d_x_post, d_b, d_c, d_cum, d_direct = ssm_backward(
        operands, state_grad, y_scan, starting, d_scanned, skip_row
    )
    d_log = span_reverse_cumulative(d_cum)
    rates = -jnp.exp(decay_log)[None, :]
    grad_decay = jnp.sum(d_log * steps * rates, axis=0)
    d_steps = d_log * rates + d_direct
    d_bc_post = jnp.concatenate([d_b, d_c], axis=-1)
    d_ext_x, grad_convx_taps, grad_convx_bias = conv_x_back(d_x_post)
    d_ext_bc, grad_convbc_taps, grad_convbc_bias = conv_bc_back(d_bc_post)
    d_pre = d_steps * jax.nn.sigmoid(step_raw + step_bias[None, :])
    grad_bias = jnp.sum(d_pre, axis=0)
    back_tails = lax.ppermute(
        jnp.concatenate([d_ext_x[:reach], d_ext_bc[:reach]], axis=1).astype(jnp.bfloat16),
        "ctx",
        backward,
    ).astype(jnp.float32)
    d_keyval = jnp.concatenate(
        [rotate(d_kv_back[:, :HEAD_SIZE], cosine, -sine), d_kv_back[:, HEAD_SIZE:]], axis=-1
    ).astype(jnp.bfloat16)
    d_queries = rotate(d_query, cos_q, -sin_q).astype(jnp.bfloat16)
    last = row_count - reach
    d_raw_x = d_ext_x[reach:].at[last:].add(back_tails[:, :xn]).astype(jnp.bfloat16)
    d_bc_part = d_ext_bc[reach:].at[last:].add(back_tails[:, xn:]).astype(jnp.bfloat16)
    d_bc_other = lax.ppermute(d_bc_part, "tp", [(0, 1), (1, 0)])
    d_bc = (d_bc_part.astype(jnp.float32) + d_bc_other.astype(jnp.float32)).astype(jnp.bfloat16)
    d_proj = jnp.concatenate(
        [d_queries, d_keyval, d_gate_z, d_raw_x, d_bc_part, d_pre.astype(jnp.bfloat16)]
        + [jnp.zeros((row_count, 2), jnp.bfloat16)],
        axis=1,
    )
    d_normed = tp_sum(contract_cols(d_proj, full_first))
    d_proj_sum = jnp.concatenate(
        [d_queries, d_keyval, d_gate_z, d_raw_x, d_bc, d_pre.astype(jnp.bfloat16)], axis=1
    )
    sum_first = scatter(contract_rows(normalized_input, d_proj_sum))
    d_from_attn, grad_gain_one = norm_back(hidden_in, scale_one, gain_one, d_normed)
    grad_tokens = (d_middle + d_from_attn).astype(jnp.bfloat16)

    tp_rank = lax.axis_index("tp")
    tp_count = lax.axis_size("tp")
    per_device = jnp.concatenate(
        [grad_convx_taps, grad_convx_bias[None]], axis=0
    ).reshape(-1)
    scalars = jnp.concatenate([grad_bias, grad_decay, grad_skip])
    own = jnp.concatenate([per_device, jnp.pad(scalars, (0, 128 - scalars.shape[0]))])
    wide = lax.dynamic_update_slice_in_dim(
        jnp.zeros((tp_count * own.shape[0],), jnp.float32), own, tp_rank * own.shape[0], 0
    )
    shared = jnp.concatenate(
        [
            grad_convbc_taps.reshape(-1),
            grad_convbc_bias,
            grad_gain_one / tp_count,
            grad_gain_two / tp_count,
        ]
    )
    sums = lax.psum(jnp.concatenate([wide, shared]), ("shard", "ctx", "tp"))
    mine = lax.dynamic_slice_in_dim(sums, tp_rank * own.shape[0], own.shape[0])
    taps_sum = mine[: (TAPS + 1) * xn].reshape(TAPS + 1, xn)
    heads_sum = mine[(TAPS + 1) * xn :]
    rest = sums[tp_count * own.shape[0] :]
    convbc_sum = rest[: (TAPS + 1) * bn].reshape(TAPS + 1, bn)
    gain_sums = rest[(TAPS + 1) * bn :].reshape(2, -1)
    gain_rows = gain_attn.shape[0]
    gain_sums = lax.dynamic_slice_in_dim(
        gain_sums, lax.axis_index("shard") * gain_rows, gain_rows, 1
    )
    out_t = sum_out.T
    return (
        result,
        grad_tokens,
        gain_sums[0],
        sum_first[:, q0:k0],
        sum_first[:, k0:z0],
        out_t[:an],
        sum_first[:, z0:x0],
        sum_first[:, x0:b0],
        sum_first[:, s0:g0],
        sum_first[:, b0:s0],
        taps_sum[:TAPS],
        taps_sum[TAPS],
        convbc_sum[:TAPS],
        convbc_sum[TAPS],
        heads_sum[:mamba_local],
        heads_sum[mamba_local : 2 * mamba_local],
        heads_sum[2 * mamba_local : 3 * mamba_local],
        out_t[an:],
        gain_sums[1],
        sum_ffn[:, :fn],
        sum_ffn[:, fn : 2 * fn],
        sum_ffn[:, 2 * fn :].T,
    )


def solution(mesh):
    return jax.shard_map(
        local,
        mesh=mesh,
        in_specs=(
            P(("shard", "ctx"), None),
            P("shard"),
            P("shard"),
            P("shard", "tp"),
            P("shard", "tp"),
            P("tp", "shard"),
            P("shard", "tp"),
            P("shard", "tp"),
            P("shard", "tp"),
            P("shard", None),
            P(None, "tp"),
            P("tp"),
            P(),
            P(),
            P("tp"),
            P("tp"),
            P("tp"),
            P("tp", "shard"),
            P("shard"),
            P("shard", "tp"),
            P("shard", "tp"),
            P("tp", "shard"),
            P(("shard", "ctx"), None),
        ),
        out_specs=(
            P(("shard", "ctx"), None),
            P(("shard", "ctx"), None),
            P("shard"),
            P("shard", "tp"),
            P("shard", "tp"),
            P("tp", "shard"),
            P("shard", "tp"),
            P("shard", "tp"),
            P("shard", "tp"),
            P("shard", None),
            P(None, "tp"),
            P("tp"),
            P(),
            P(),
            P("tp"),
            P("tp"),
            P("tp"),
            P("tp", "shard"),
            P("shard"),
            P("shard", "tp"),
            P("shard", "tp"),
            P("tp", "shard"),
        ),
        check_vma=False,
    )
```

time: 1480 us -> 636 us (0.43)
  matrix products: 282 us -> 47.8 us
  waiting for transfers between devices: 475 us -> 260 us
  local copies, waits for them, and re-layouts: 249 us -> 69.7 us
  blocking collectives: 249 us -> 106 us
  other arithmetic: 172 us -> 63.5 us
  Pallas kernels: 0 us -> 54.4 us
    dot_general x90 -> x6, matrix products: 222 us -> 19.5 us  [the longest x1 7.27 us: local(): gate_up = jnp.dot(normed_ffn, full_ffn, preferred_element_type=jnp.float32)]
    reduce_scatter x11 -> x3, waiting for transfers between devices: 317 us -> 115 us  [scatter(): lax.psum_scatter(values.astype(jnp.bfloat16), 'shard', scatter_dimension=...]
    dynamic_update_slice x65 -> x0, local copies, waits for them, and re-layouts: 130 us -> none  [the longest x60 129 us: ssm_local(): lax.scan(partial(span_step, decay_rates), initial, (to_blocks(inputs), to...]
    all_gather x12 -> x3, blocking collectives: 159 us -> 60.3 us  [the longest x1 27.1 us: local(): d_state_parts = lax.all_gather(d_state_local.astype(jnp.bfloat16), 'ctx')]
    pallas_call x0 -> x6, Pallas kernels: none -> 54.4 us  [the longest x1 17.3 us: attn_backward(): pl.pallas_call(partial(attn_bwd_kernel, heads), grid=(count // QUERY_ROWS...]
    unnamed x3 -> x0, blocking collectives: 37.1 us -> none
    dynamic_update_slice x26 -> x1, other arithmetic: 33.1 us -> 0.13 us  [local(): lax.dynamic_update_slice_in_dim(jnp.zeros((tp_count * own.shape[0],), jnp...]
    psum x4 -> x1, waiting for transfers between devices: 91.8 us -> 63.7 us  [scatter(): return lax.psum(part, 'ctx').astype(jnp.float32)]
  transfers between devices with their start and end apart: 22 -> 16, of which waited for: 14 -> 8; matrix products, arithmetic and copies ran while one was open for 26% -> 19% of each run, Pallas kernels for 0% -> 6%
where the time goes in v1:
time: 636 us; the launch traced here: 625 us
  waiting for transfers between devices  260 us (41%)
  blocking collectives  106 us (17%)
  local copies, waits for them, and re-layouts  69.7 us (11%)
  other arithmetic  63.5 us (10%)
  Pallas kernels  54.4 us (9%)
  matrix products  47.8 us (8%)
  between operations  18.1 us (3%)
    reduce_scatter x3, waiting for transfers between devices, scatter(): lax.psum_scatter(values.astype(jnp.bfloat16), 'shard', scatter_dimension=...  115 us
    psum x1, waiting for transfers between devices, scatter(): return lax.psum(part, 'ctx').astype(jnp.float32)  63.7 us
    all_gather x1, waiting for transfers between devices, local(): full_first = lax.all_gather(first_pack, 'shard', axis=0, tiled=True)  48.9 us
    psum x1, blocking collectives, local(): sums = lax.psum(jnp.concatenate([wide, shared]), ('shard', 'ctx', 'tp'))  45.7 us
    unnamed x358, local copies, waits for them, and re-layouts  29.5 us
    all_gather x1, blocking collectives, local(): d_state_parts = lax.all_gather(d_state_local.astype(jnp.bfloat16), 'ctx')  27.1 us
    all_gather x1, waiting for transfers between devices, local(): full_down = lax.all_gather(w_down.T, 'shard', axis=0, tiled=True)  26.3 us
    all_gather x1, blocking collectives, local(): lax.all_gather(jnp.concatenate([local_state, through_row], axis=0).astype...  17.5 us
  transfers between devices with their start and end apart: 16, of which 8 were waited for; matrix products, arithmetic and copies ran while one was open for 19% of the time, Pallas kernels for 6%

profile of v1, /device:TPU:0, one launch (start us, length us, event | category | flops | bytes accessed | tf_op | source)
XLA Modules:
  0.0 625.1 jit_solution(4584129856505489373)
XLA Ops:
  24.0 48.9 %all-gather.6.cloned.1.call-done = bf16[1024,2190]{1,0:T(8,128)(2,1)} async-done(((bf16[256,2190]{1,0:T(8,128)(2,1)}), bf16[1024,2190]{1,0:T(8,128)(2,1)}) %all-gather.6.cloned.1.call-update) | async-done | bytes 4485136 | tf_op jit(solution)/shard_map/all_gather | solution.py:498
  74.5 5.0 fusion.94
  87.4 15.7 %all_gather.26.kv_ref = bf16[2048,128]{1,0:T(8,128)(2,1)S(1)} all-gather(bf16[512,128]{1,0:T(8,128)(2,1)S(1)} %pad_maximum_fusion.8), channel_id=1, replica_groups=mesh['shard'=4,'ctx'=4,'tp'=2] {'ctx'}, dimensions={0}, use_global_device_ids=true | all-gather | bytes 655360 | tf_op jit(solution)/shard_map/all_gather | solution.py:541
  105.1 11.1 %attn_forward.1 = (f32[512,256]{1,0:T(8,128)S(1)}, f32[2048,1]{1,0:T(8,128)S(1)}) custom-call(bf16[512,256]{1,0:T(8,128)(2,1)S(1)} %get-tuple-element.294.q_ref, bf16[2048,128]{1,0:T(8,128)(2,1)S(1)} %all_gather.26.kv_ref, s32[512,1]{1,0:T(8,128)S(1)} %copy.189.low_ref, s32[512,1]{1,0:T(8,128)S(1)} %iota_add_fusion.high_ref), custom_call_target="tpu_custom_call" | custom-call | flops 1073741824 | bytes 524288 | tf_op jit(solution)/shard_map/attn_forward/pallas_call | solution.py:162
  124.2 17.5 %all_gather.27 = bf16[4,784,128]{2,1,0:T(8,128)(2,1)S(1)} all-gather(bf16[1,784,128]{2,1,0:T(8,128)(2,1)S(1)} %fusion.57), channel_id=1, replica_groups=mesh['shard'=4,'ctx'=4,'tp'=2] {'ctx'}, dimensions={0}, use_global_device_ids=true | all-gather | bytes 1003520 | tf_op jit(solution)/shard_map/all_gather | solution.py:566
  149.0 7.1 %ssm_forward.1 = (f32[512,768]{1,0:T(8,128)S(1)}, f32[4,768,128]{2,1,0:T(8,128)S(1)}) custom-call(f32[512,768]{1,0:T(8,128)} %copy-done, bf16[512,128]{1,0:T(8,128)(2,1)S(1)} %copy-done.14, bf16[512,128]{1,0:T(8,128)(2,1)S(1)} %get-tuple-element.274.c_ref.m_ref, f32[512,12]{1,0:T(8,128)S(1)} %copy-done.5, f32[512,12]{1,0:T(8,128)S(1)} %bitcast.160, ...), custom_call_target="tpu_custom_call" | custom-call | tf_op jit(solution)/shard_map/ssm_forward/pallas_call | solution.py:380
  157.3 3.8 multiply_convert_fusion.2
  169.0 7.3 %fusion.77 = f32[512,2048]{1,0:T(8,128)} fusion(bf16[1024,2048]{1,0:T(8,128)(2,1)} %all-gather.10.cloned.1.call-done, f32[512,1024]{1,0:T(8,128)} %get-tuple-element.224, f32[1024]{0:T(1024)S(1)} %get-tuple-element.204, f32[512]{0:T(512)S(1)} %get-tuple-element.304), kind=kOutput, calls=%fused_computation.258 | convolution fusion | flops 2149056512 | bytes 10491904 | tf_op jit(solution)/shard_map/dot_general | solution.py:587
  176.3 26.3 %all-gather.12.cloned.1.call-done = bf16[1024,1024]{0,1:T(8,128)(2,1)} async-done(((bf16[256,1024]{0,1:T(8,128)(2,1)}), bf16[1024,1024]{0,1:T(8,128)(2,1)}) %all-gather.12.cloned.1.call-update) | async-done | bytes 2097168 | tf_op jit(solution)/shard_map/all_gather | solution.py:501
  202.6 5.0 fusion.1
  218.0 4.0 subtract_add_fusion
  224.3 4.4 multiply_reduce_fusion.3
  228.7 17.3 %attn_backward.1 = (f32[512,256]{1,0:T(8,128)S(1)}, f32[2048,128]{1,0:T(8,128)S(1)}) custom-call(bf16[512,256]{1,0:T(8,128)(2,1)S(1)} %copy-done.31, bf16[2048,128]{1,0:T(8,128)(2,1)S(1)} %copy-done.19, s32[512,1]{1,0:T(8,128)S(1)} %copy-done.27, s32[512,1]{1,0:T(8,128)S(1)} %copy-done.25, f32[512,256]{1,0:T(8,128)S(1)} %copy-done.21, ...), custom_call_target="tpu_custom_call" | custom-call | flops 2684354560 | bytes 1048576 | tf_op jit(solution)/shard_map/attn_backward/pallas_call | solution.py:185
  248.7 27.1 %all-gather = bf16[3072,128]{1,0:T(8,128)(2,1)S(1)} all-gather(bf16[768,128]{1,0:T(8,128)(2,1)S(1)} %convert_element_type.263), channel_id=2, replica_groups=mesh['shard'=4,'ctx'=4,'tp'=2] {'ctx'}, dimensions={0}, use_global_device_ids=true | all-gather | bytes 983040 | tf_op jit(solution)/shard_map/all_gather | solution.py:626
  276.3 15.8 %ssm_backward.1 = (f32[512,768]{1,0:T(8,128)S(1)}, f32[512,128]{1,0:T(8,128)S(1)}, f32[512,128]{1,0:T(8,128)S(1)}, f32[512,12]{1,0:T(8,128)S(1)}, f32[512,12]{1,0:T(8,128)S(1)}) custom-call(f32[512,768]{1,0:T(8,128)S(1)} %copy-done.1, bf16[512,128]{1,0:T(8,128)(2,1)S(1)} %copy-done.15, bf16[512,128]{1,0:T(8,128)(2,1)S(1)} %get-tuple-element.274.c_ref.m_ref, ...), custom_call_target="tpu_custom_call" | custom-call | tf_op jit(solution)/shard_map/ssm_backward/pallas_call | solution.py:399
  300.2 6.1 multiply_reduce_fusion.7
  327.8 4.1 concatenate.143
  331.9 6.4 %convolution_convert_fusion = bf16[1024,2188]{0,1:T(8,128)(2,1)} fusion(bf16[512,2188]{1,0:T(8,128)(2,1)} %concatenate.143, bf16[512,1024]{1,0:T(8,128)(2,1)S(1)} %copy-done.43, f32[1024]{0:T(1024)S(1)} %copy-done.97, f32[512]{0:T(512)S(1)} %copy-done.111), kind=kOutput, calls=%fused_computation.1 | convolution fusion | flops 2298621952 | bytes 7776256 | tf_op jit(solution)/shard_map/dot_general | solution.py:36
  348.7 4.5 concatenate.138
  353.1 41.5 %reduce-scatter.7.cloned.1.call-done = bf16[256,2188]{0,1:T(8,128)(2,1)} async-done(((bf16[1024,2188]{0,1:T(8,128)(2,1)}), bf16[256,2188]{0,1:T(8,128)(2,1)}) %reduce-scatter.7.cloned.1.call-update) | async-done | bytes 1120272 | tf_op jit(solution)/shard_map/reduce_scatter | solution.py:609
  394.7 73.2 %reduce-scatter.11.cloned.1.call-done = bf16[256,3072]{1,0:T(8,128)(2,1)} async-done(((bf16[1024,3072]{1,0:T(8,128)(2,1)}), bf16[256,3072]{1,0:T(8,128)(2,1)}) %reduce-scatter.11.cloned.1.call-update) | async-done | bytes 1572880 | tf_op jit(solution)/shard_map/reduce_scatter | solution.py:609
  468.0 5.9 convolution_convert_fusion.3
  479.5 45.7 %psum.28 = f32[11264]{0:T(1024)S(1)} all-reduce(f32[11264]{0:T(1024)S(1)} %constant_dynamic-update-slice_fusion.3), channel_id=1, replica_groups=mesh['shard'=4,'ctx'=4,'tp'=2] {'shard','ctx','tp'}, use_global_device_ids=true, to_apply=%region_23.24 | all-reduce | flops 11264 | bytes 90112 | tf_op jit(solution)/shard_map/psum | solution.py:690
  532.2 63.7 %all-reduce.22.cloned.1.call-done = (bf16[256,2188]{0,1:T(8,128)(2,1)}, bf16[1024,256]{0,1:T(8,128)(2,1)}, bf16[256,3072]{1,0:T(8,128)(2,1)}) async-done(((bf16[256,2188]{0,1:T(8,128)(2,1)}, bf16[1024,256]{0,1:T(8,128)(2,1)}, bf16[256,3072]{1,0:T(8,128)(2,1)}), (bf16[256,2188]{0,1:T(8,128)(2,1)}, bf16[1024,256]{0,1:T(8,128)(2,1)}, bf16[256,3072]{1,0:T(8,128)(2,1)})) %all-reduce.22.cloned.1.call-update) | async-done | bytes 3217424 | tf_op jit(solution)/shard_map/psum | solution.py:612
  (567 shorter events, 139.6 us)
Async XLA Ops:
  7.2 65.7 %all-gather.6.cloned.1.call-start = ((), (), s32[]{:S(2)}) async-start(), calls=%async_computation.4 | async-start | bytes 5898240 | tf_op jit(solution)/shard_map/all_gather | solution.py:498
  12.9 148.2 %all-gather.8.cloned.1.call-start = ((), (), s32[]{:S(2)}) async-start(), calls=%async_computation.5 | async-start | bytes 2621440 | tf_op jit(solution)/shard_map/all_gather | solution.py:499
  13.9 155.1 %all-gather.10.cloned.1.call-start = ((), (), s32[]{:S(2)}) async-start(), calls=%async_computation.6 | async-start | bytes 5242880 | tf_op jit(solution)/shard_map/all_gather | solution.py:500
  15.1 187.5 %all-gather.12.cloned.1.call-start = ((), (), s32[]{:S(2)}) async-start(), calls=%async_computation.7 | async-start | bytes 2621440 | tf_op jit(solution)/shard_map/all_gather | solution.py:501
  15.6 307.0 %reduce-scatter.5.cloned.1.call-start = ((), (), s32[]{:S(2)}) async-start(), calls=%async_computation.8 | async-start | bytes 655360 | tf_op jit(solution)/shard_map/reduce_scatter | solution.py:628
  21.2 97.6 %copy-start.98 = (pred[512]{0:T(512)(128)(4,1)}, pred[512]{0:T(512)(128)(4,1)S(1)}, u32[]{:S(2)}) copy-start(pred[512]{0:T(512)(128)(4,1)S(1)} %get-tuple-element.289) | copy-start | bytes 1540
  21.2 97.6 %copy-start.101 = (pred[512]{0:T(512)(128)(4,1)}, pred[512]{0:T(512)(128)(4,1)S(1)}, u32[]{:S(2)}) copy-start(pred[512]{0:T(512)(128)(4,1)S(1)} %get-tuple-element.290) | copy-start | bytes 1540
  21.2 97.6 %copy-start.104 = (pred[512]{0:T(512)(128)(4,1)}, pred[512]{0:T(512)(128)(4,1)S(1)}, u32[]{:S(2)}) copy-start(pred[512]{0:T(512)(128)(4,1)S(1)} %get-tuple-element.291) | copy-start | bytes 1540
  21.2 97.5 %copy-start.124 = (f32[1,256]{1,0:T(1,128)}, f32[1,256]{1,0:T(1,128)S(1)}, u32[]{:S(2)}) copy-start(f32[1,256]{1,0:T(1,128)S(1)} %get-tuple-element.285) | copy-start | bytes 3076
  21.2 97.5 %copy-start.126 = (f32[1,256]{1,0:T(1,128)}, f32[1,256]{1,0:T(1,128)S(1)}, u32[]{:S(2)}) copy-start(f32[1,256]{1,0:T(1,128)S(1)} %get-tuple-element.286) | copy-start | bytes 3076
  21.3 97.5 %copy-start.128 = (f32[1,256]{1,0:T(1,128)}, f32[1,256]{1,0:T(1,128)S(1)}, u32[]{:S(2)}) copy-start(f32[1,256]{1,0:T(1,128)S(1)} %get-tuple-element.287) | copy-start | bytes 3076
  74.5 143.5 %copy-start.84 = (f32[1024]{0:T(1024)}, f32[1024]{0:T(1024)S(1)}, u32[]{:S(2)}) copy-start(f32[1024]{0:T(1024)S(1)} %get-tuple-element.204) | copy-start | bytes 12292
  80.6 38.0 %collective-permute-start = (bf16[3,1024]{1,0:T(4,128)(2,1)S(1)}, bf16[3,1024]{1,0:T(4,128)(2,1)S(1)}, u32[]{:S(2)}, u32[]{:S(2)}) collective-permute-start(bf16[3,1024]{1,0:T(4,128)(2,1)S(1)} %slice.623), channel_id=1, source_target_pairs={{0,2},{2,4},{4,6},{1,3},{3,5},{5,7},{8,10},{10,12},{12,14},{9,11},... | collective-permute-start | bytes 18440 | tf_op jit(solution)/shard_map/ppermute | solution.py:536
  164.4 2.7 collective-permute-start.1
  210.0 4.5 collective-permute-start.3
  212.6 5.4 collective-permute-start.2
  247.0 106.2 %reduce-scatter.9.cloned.1.call-start = ((), (), s32[]{:S(2)}) async-start(), calls=%async_computation.10 | async-start | bytes 2621440 | tf_op jit(solution)/shard_map/reduce_scatter | solution.py:609
  299.6 95.1 %reduce-scatter.7.cloned.1.call-start = ((), (), s32[]{:S(2)}) async-start(), calls=%async_computation.9 | async-start | bytes 5611520 | tf_op jit(solution)/shard_map/reduce_scatter | solution.py:609
  308.5 5.5 collective-permute-start.4
  314.3 6.4 %collective-permute-start.6 = (bf16[512,256]{1,0:T(8,128)(2,1)S(1)}, bf16[512,256]{1,0:T(8,128)(2,1)}, u32[]{:S(2)}, u32[]{:S(2)}) collective-permute-start(bf16[512,256]{1,0:T(8,128)(2,1)S(1)} %scatter-add.9), channel_id=1, source_target_pairs={{0,1},{1,0},{2,3},{3,2},{4,5},{5,4},{6,7},{7,6},{8,9},{9,8},{10,11... | collective-permute-start | bytes 786440 | tf_op jit(solution)/shard_map/ppermute | solution.py:657
  338.3 129.5 %reduce-scatter.11.cloned.1.call-start = ((), (), s32[]{:S(2)}) async-start(), calls=%async_computation.11 | async-start | bytes 7864320 | tf_op jit(solution)/shard_map/reduce_scatter | solution.py:609
  347.2 248.8 %all-reduce.22.cloned.1.call-start = ((), (), s32[]{:S(2)}) async-start(), calls=%async_computation.12 | async-start | bytes 6438912 | tf_op jit(solution)/shard_map/psum | solution.py:612
  353.1 114.8 %copy-start.63 = (bf16[512,2190]{1,0:T(8,128)(2,1)S(1)}, bf16[512,2190]{1,0:T(8,128)(2,1)}, u32[]{:S(2)}) copy-start(bf16[512,2190]{1,0:T(8,128)(2,1)} %concatenate.138) | copy-start | bytes 6727684
  474.0 3.0 collective-permute-start.5
  (164 other events, 2106.5 us)
Sparse Core Ops, SparseCore 0:
  13.0 59.7 all-gather.5
  75.3 35.1 all-gather.7
  112.9 52.6 all-gather.9
  167.3 35.1 all-gather.11
  247.1 25.6 reduce-scatter.4
  299.7 34.4 reduce-scatter.8
  338.4 56.1 reduce-scatter.6
  397.6 70.1 reduce-scatter.10
  470.5 125.4 all-reduce.21

commit v2 on v1

--- a/solution.py
+++ b/solution.py
@@ -91,6 +91,73 @@
     low = values.astype(jnp.bfloat16)
     other = lax.ppermute(low, "tp", [(0, 1), (1, 0)])
     return low.astype(jnp.float32) + other.astype(jnp.float32)
+
+
+def partners(axis, bit):
+    return [(k, k ^ bit) for k in range(lax.axis_size(axis))]
+
+
+def bits_of(axis):
+    bit, bits = lax.axis_size(axis) // 2, []
+    while bit:
+        bits.append(bit)
+        bit //= 2
+    return bits
+
+
+def gather_rows(block, axis):
+    count, me = (lax.axis_size(axis), lax.axis_index(axis))
+    rows = block.shape[0]
+    half = rows // 2
+    full = jnp.zeros((count * rows, block.shape[1]), block.dtype)
+    for part, bits in enumerate((bits_of(axis), bits_of(axis)[::-1])):
+        pieces = {0: block[part * half : (part + 1) * half]}
+        for bit in bits:
+            for offset in list(pieces):
+                pieces[offset ^ bit] = lax.ppermute(pieces[offset], axis, partners(axis, bit))
+        for offset, piece in pieces.items():
+            place = (me ^ offset) * rows + part * half
+            full = lax.dynamic_update_slice_in_dim(full, piece, place, 0)
+    return full
+
+
+def reduce_rows(values, axis):
+    count, me = (lax.axis_size(axis), lax.axis_index(axis))
+    half = values.shape[0] // count // 2
+    bits = bits_of(axis)
+    parts = []
+    for part, order in enumerate((bits, bits[::-1])):
+        total = values.reshape((2,) * len(bits) + (2, half, values.shape[1]))
+        total = lax.index_in_dim(total, part, len(bits), False)
+        left = list(bits)
+        for bit in order:
+            dim = left.index(bit)
+            left.remove(bit)
+            own = (me // bit) % 2
+            sent = lax.dynamic_index_in_dim(total, 1 - own, dim, False).astype(jnp.bfloat16)
+            kept = lax.dynamic_index_in_dim(total, own, dim, False).astype(jnp.float32)
+            got = lax.ppermute(sent, axis, partners(axis, bit)).astype(jnp.float32)
+            total = (kept + got).astype(jnp.bfloat16)
+        parts.append(total)
+    return jnp.concatenate(parts, axis=0)
+
+
+def sum_over(values, axes):
+    for axis in axes:
+        for bit in bits_of(axis):
+            values = values + lax.ppermute(values, axis, partners(axis, bit))
+    return values
+
+
+def shifted(values, step):
+    count = lax.axis_size("ctx")
+    pairs = [(k, k + step) for k in range(count) if 0 <= k + step < count]
+    return lax.ppermute(values, "ctx", pairs)
+
+
+def place_from(step):
+    count = lax.axis_size("ctx")
+    return lax.rem(lax.axis_index("ctx") - step + count, count)
 
 
 def stack_heads(block, heads):
@@ -462,16 +529,27 @@
     )
 
 
-def join_states(states, through, forward):
-    length, place = (lax.axis_size("ctx"), lax.axis_index("ctx"))
-    order = range(length - 1, -1, -1) if forward else range(length)
-    factor = jnp.ones_like(through[0])
-    total = jnp.zeros(states.shape[1:], jnp.float32)
-    for k in order:
-        reached = (k < place) if forward else (k > place)
-        weight = jnp.repeat(jnp.where(reached, factor, 0.0), MP)
-        total = total + weight[:, None] * states[k].astype(jnp.float32)
-        factor = jnp.where(reached, factor * through[k], factor)
+def earlier_states(states, through):
+    payload = jnp.concatenate([states, through], axis=0).astype(jnp.bfloat16)
+    inner, heads = states.shape[0], states.shape[0] // MP
+    total = jnp.zeros(states.shape, jnp.float32)
+    factor = jnp.ones((heads,), jnp.float32)
+    for step in range(1, lax.axis_size("ctx")):
+        got = shifted(payload, step)
+        total = total + jnp.repeat(factor, MP)[:, None] * got[:inner].astype(jnp.float32)
+        factor = factor * got[inner, :heads].astype(jnp.float32)
+    return total
+
+
+def later_states(d_states, through):
+    payload = jnp.concatenate([d_states, through], axis=0).astype(jnp.bfloat16)
+    inner, heads = d_states.shape[0], d_states.shape[0] // MP
+    total = jnp.zeros(d_states.shape, jnp.float32)
+    factor = jnp.ones((heads,), jnp.float32)
+    for step in range(1, lax.axis_size("ctx")):
+        got = shifted(payload, -step)
+        total = total + jnp.repeat(factor, MP)[:, None] * got[:inner].astype(jnp.float32)
+        factor = factor * got[inner, :heads].astype(jnp.float32)
     return total
 
 
@@ -495,10 +573,13 @@
     )
     out_pack = jnp.concatenate([w_attn_out, w_ssm_out], axis=0).T
     ffn_pack = jnp.concatenate([w_gate, w_up], axis=1)
-    full_first = lax.all_gather(first_pack, "shard", axis=0, tiled=True)
-    full_out = lax.all_gather(out_pack, "shard", axis=0, tiled=True)
+    full_first = gather_rows(first_pack, "shard")
+    full_first, out_pack, ffn_pack, down_pack = lax.optimization_barrier(
+        (full_first, out_pack, ffn_pack, w_down.T)
+    )
+    full_out = gather_rows(out_pack, "shard")
     full_ffn = lax.all_gather(ffn_pack, "shard", axis=0, tiled=True)
-    full_down = lax.all_gather(w_down.T, "shard", axis=0, tiled=True)
+    full_down = lax.all_gather(down_pack, "shard", axis=0, tiled=True)
 
     row_count = tokens.shape[0]
     ctx_rank = lax.axis_index("ctx")
@@ -538,7 +619,12 @@
         "ctx",
         onward,
     )
-    all_keys = lax.all_gather(keyval, "ctx", axis=0, tiled=True)
+    all_keys = jnp.zeros((ctx_count * row_count, keyval.shape[1]), keyval.dtype)
+    all_keys = lax.dynamic_update_slice_in_dim(all_keys, keyval, first_row, 0)
+    for step in range(1, ctx_count):
+        all_keys = lax.dynamic_update_slice_in_dim(
+            all_keys, shifted(keyval, step), place_from(step) * row_count, 0
+        )
 
     ext_x = jnp.concatenate([tails[:, :xn], raw_x], axis=0).astype(jnp.float32)
     ext_bc = jnp.concatenate([tails[:, xn:], raw_bc], axis=0).astype(jnp.float32)
@@ -563,13 +649,9 @@
     )
     local_state = weighted_outer(conv_x, steps * ending_all, b_low)
     through_row = jnp.zeros((16, NS), jnp.float32).at[0, :mamba_local].set(through)
-    state_parts = lax.all_gather(
-        jnp.concatenate([local_state, through_row], axis=0).astype(jnp.bfloat16), "ctx"
-    )
+    state_in = earlier_states(local_state, through_row)
     attn_out, lse = attn_forward(queries, all_keys, low, high)
     attended = attn_out.astype(jnp.bfloat16)
-    all_through = state_parts[:, xn, :mamba_local].astype(jnp.float32)
-    state_in = join_states(state_parts[:, :xn], all_through, True)
     operands = (
         conv_x, b_low, c_low, steps, cum, cum.T, entry, ending, seg_local[:, None],
         seg_local[None, :],
@@ -605,13 +687,16 @@
     grad_down_t = contract_rows(grad_out, active)
     grad_ffn = contract_rows(normed_ffn, d_gate_up)
 
-    def scatter(values):
-        part = lax.psum_scatter(
-            values.astype(jnp.bfloat16), "shard", scatter_dimension=0, tiled=True
-        )
-        return lax.psum(part, "ctx").astype(jnp.float32)
-
-    sum_ffn = scatter(jnp.concatenate([grad_ffn, grad_down_t], axis=1))
+    def scatter(values, after):
+        part = reduce_rows(values, "shard")
+        if after is not None:
+            part, after = lax.optimization_barrier((part, after))
+        return lax.psum(part, "ctx")
+
+    sum_ffn = scatter(
+        jnp.concatenate([grad_ffn.astype(jnp.bfloat16), grad_down_t.astype(jnp.bfloat16)], axis=1),
+        None,
+    )
 
     d_from_ffn, grad_gain_two = norm_back(middle, scale_two, gain_two, d_normed_ffn)
     d_middle = grad_out.astype(jnp.float32) + d_from_ffn
@@ -623,13 +708,19 @@
     d_gate_z = (d_gated * scanned * silu_slope(gate_z)).astype(jnp.bfloat16)
     grad_skip = jnp.sum((d_scanned * conv_x).reshape(row_count, mamba_local, MP), axis=(0, 2))
     d_state_local = weighted_outer(d_scanned, entry_all, c_low)
-    d_state_parts = lax.all_gather(d_state_local.astype(jnp.bfloat16), "ctx")
+    state_grad = later_states(d_state_local, through_row)
     d_query, d_kv_group = attn_backward(queries, all_keys, low, high, attn_out, lse, d_attended)
-    d_kv_back = lax.psum_scatter(
-        d_kv_group.astype(jnp.bfloat16), "ctx", scatter_dimension=0, tiled=True
-    ).astype(jnp.float32)
-    sum_out = scatter(contract_rows(d_mid_low, mixer))
-    state_grad = join_states(d_state_parts, all_through, False)
+    d_kv_back = lax.dynamic_slice_in_dim(d_kv_group, first_row, row_count)
+    for step in range(1, ctx_count):
+        part = lax.dynamic_slice_in_dim(d_kv_group, place_from(step) * row_count, row_count)
+        d_kv_back = d_kv_back + shifted(part.astype(jnp.bfloat16), -step).astype(jnp.float32)
+    sum_out = scatter(contract_rows(d_mid_low, mixer).astype(jnp.bfloat16), sum_ffn)
+    d_keyval = jnp.concatenate(
+        [rotate(d_kv_back[:, :HEAD_SIZE], cosine, -sine), d_kv_back[:, HEAD_SIZE:]], axis=-1
+    ).astype(jnp.bfloat16)
+    d_queries = rotate(d_query, cos_q, -sin_q).astype(jnp.bfloat16)
+    d_early = jnp.concatenate([d_queries, d_keyval, d_gate_z], axis=1)
+    sum_early = scatter(contract_rows(normalized_input, d_early).astype(jnp.bfloat16), sum_out)
     d_x_post, d_b, d_c, d_cum, d_direct = ssm_backward(
         operands, state_grad, y_scan, starting, d_scanned, skip_row
     )
@@ -647,69 +738,60 @@
         "ctx",
         backward,
     ).astype(jnp.float32)
-    d_keyval = jnp.concatenate(
-        [rotate(d_kv_back[:, :HEAD_SIZE], cosine, -sine), d_kv_back[:, HEAD_SIZE:]], axis=-1
-    ).astype(jnp.bfloat16)
-    d_queries = rotate(d_query, cos_q, -sin_q).astype(jnp.bfloat16)
     last = row_count - reach
     d_raw_x = d_ext_x[reach:].at[last:].add(back_tails[:, :xn]).astype(jnp.bfloat16)
     d_bc_part = d_ext_bc[reach:].at[last:].add(back_tails[:, xn:]).astype(jnp.bfloat16)
     d_bc_other = lax.ppermute(d_bc_part, "tp", [(0, 1), (1, 0)])
     d_bc = (d_bc_part.astype(jnp.float32) + d_bc_other.astype(jnp.float32)).astype(jnp.bfloat16)
-    d_proj = jnp.concatenate(
-        [d_queries, d_keyval, d_gate_z, d_raw_x, d_bc_part, d_pre.astype(jnp.bfloat16)]
-        + [jnp.zeros((row_count, 2), jnp.bfloat16)],
-        axis=1,
-    )
-    d_normed = tp_sum(contract_cols(d_proj, full_first))
-    d_proj_sum = jnp.concatenate(
-        [d_queries, d_keyval, d_gate_z, d_raw_x, d_bc, d_pre.astype(jnp.bfloat16)], axis=1
-    )
-    sum_first = scatter(contract_rows(normalized_input, d_proj_sum))
+    d_steps_low = d_pre.astype(jnp.bfloat16)
+    d_late = jnp.concatenate(
+        [d_raw_x, d_bc_part, d_steps_low, jnp.zeros((row_count, 2), jnp.bfloat16)], axis=1
+    )
+    d_normed = tp_sum(
+        contract_cols(d_early, full_first[:, :x0]) + contract_cols(d_late, full_first[:, x0:])
+    )
+    d_late_sum = jnp.concatenate([d_raw_x, d_bc, d_steps_low], axis=1)
+    sum_late = scatter(contract_rows(normalized_input, d_late_sum).astype(jnp.bfloat16), sum_early)
     d_from_attn, grad_gain_one = norm_back(hidden_in, scale_one, gain_one, d_normed)
     grad_tokens = (d_middle + d_from_attn).astype(jnp.bfloat16)
 
-    tp_rank = lax.axis_index("tp")
-    tp_count = lax.axis_size("tp")
-    per_device = jnp.concatenate(
-        [grad_convx_taps, grad_convx_bias[None]], axis=0
-    ).reshape(-1)
     scalars = jnp.concatenate([grad_bias, grad_decay, grad_skip])
-    own = jnp.concatenate([per_device, jnp.pad(scalars, (0, 128 - scalars.shape[0]))])
-    wide = lax.dynamic_update_slice_in_dim(
-        jnp.zeros((tp_count * own.shape[0],), jnp.float32), own, tp_rank * own.shape[0], 0
-    )
-    shared = jnp.concatenate(
+    gain_grads = jnp.concatenate([grad_gain_one, grad_gain_two])
+    own = jnp.concatenate(
         [
+            grad_convx_taps.reshape(-1),
+            grad_convx_bias,
+            jnp.pad(scalars, (0, 128 - scalars.shape[0])),
+            gain_grads,
             grad_convbc_taps.reshape(-1),
             grad_convbc_bias,
-            grad_gain_one / tp_count,
-            grad_gain_two / tp_count,
         ]
-    )
-    sums = lax.psum(jnp.concatenate([wide, shared]), ("shard", "ctx", "tp"))
-    mine = lax.dynamic_slice_in_dim(sums, tp_rank * own.shape[0], own.shape[0])
-    taps_sum = mine[: (TAPS + 1) * xn].reshape(TAPS + 1, xn)
-    heads_sum = mine[(TAPS + 1) * xn :]
-    rest = sums[tp_count * own.shape[0] :]
-    convbc_sum = rest[: (TAPS + 1) * bn].reshape(TAPS + 1, bn)
-    gain_sums = rest[(TAPS + 1) * bn :].reshape(2, -1)
+    ).reshape(-1, 128)
+    own = sum_over(own, ("shard", "ctx")).reshape(-1)
+    taps_sum = own[: (TAPS + 1) * xn].reshape(TAPS + 1, xn)
+    heads_sum = own[(TAPS + 1) * xn : (TAPS + 1) * xn + 128]
+    shared = own[(TAPS + 1) * xn + 128 :]
+    gain_sums = shared[: gain_grads.shape[0]].reshape(2, -1)
+    convbc_sum = sum_over(shared[gain_grads.shape[0] :].reshape(-1, 128), ("tp",))
+    convbc_sum = convbc_sum.reshape(TAPS + 1, bn)
     gain_rows = gain_attn.shape[0]
     gain_sums = lax.dynamic_slice_in_dim(
         gain_sums, lax.axis_index("shard") * gain_rows, gain_rows, 1
     )
+    sum_ffn, sum_out = sum_ffn.astype(jnp.float32), sum_out.astype(jnp.float32)
+    sum_early, sum_late = sum_early.astype(jnp.float32), sum_late.astype(jnp.float32)
     out_t = sum_out.T
     return (
         result,
         grad_tokens,
         gain_sums[0],
-        sum_first[:, q0:k0],
-        sum_first[:, k0:z0],
+        sum_early[:, q0:k0],
+        sum_early[:, k0:z0],
         out_t[:an],
-        sum_first[:, z0:x0],
-        sum_first[:, x0:b0],
-        sum_first[:, s0:g0],
-        sum_first[:, b0:s0],
+        sum_early[:, z0:x0],
+        sum_late[:, : b0 - x0],
+        sum_late[:, s0 - x0 :],
+        sum_late[:, b0 - x0 : s0 - x0],
         taps_sum[:TAPS],
         taps_sum[TAPS],
         convbc_sum[:TAPS],

time: 636 us -> 642 us (level)
  blocking collectives: 106 us -> 0 us
  starting transfers between devices: 5.58 us -> 59.1 us
  local copies, waits for them, and re-layouts: 69.7 us -> 123 us
  other arithmetic: 63.5 us -> 85.7 us
  waiting for transfers between devices: 260 us -> 243 us
    reduce_scatter x4 -> x0, waiting for transfers between devices: 115 us -> none  [the longest x3 115 us: scatter(): lax.psum_scatter(values.astype(jnp.bfloat16), 'shard', scatter_dimension=...]
    psum x1 -> x4, waiting for transfers between devices: 63.7 us -> 155 us  [scatter(): return lax.psum(part, 'ctx')]
    ppermute x0 -> x45, waiting for transfers between devices: none -> 82 us  [the longest x16 31.7 us: reduce_rows(): got = lax.ppermute(sent, axis, partners(axis, bit)).astype(jnp.float32)]
    all_gather x3 -> x1, waiting for transfers between devices: 75.2 us -> 0.73 us  [local(): full_down = lax.all_gather(down_pack, 'shard', axis=0, tiled=True)]
    all_gather x3 -> x0, blocking collectives: 60.3 us -> none  [the longest x1 27.1 us: local(): d_state_parts = lax.all_gather(d_state_local.astype(jnp.bfloat16), 'ctx')]
    ppermute x0 -> x45, starting transfers between devices: none -> 55.2 us  [the longest x12 21.9 us: shifted(): return lax.ppermute(values, 'ctx', pairs)]
    psum x1 -> x0, blocking collectives: 45.7 us -> none  [local(): sums = lax.psum(jnp.concatenate([wide, shared]), ('shard', 'ctx', 'tp'))]
    squeeze x0 -> x14, local copies, waits for them, and re-layouts: none -> 16.4 us  [the longest x12 15.3 us: reduce_rows(): lax.dynamic_index_in_dim(total, 1 - own, dim, False).astype(jnp.bfloat16)]
  transfers between devices with their start and end apart: 16 -> 58, of which waited for: 8 -> 20; matrix products, arithmetic and copies ran while one was open for 19% -> 36% of each run, Pallas kernels for 6% -> 9%
where the time goes in v2:
time: 642 us; the launch traced here: 634 us
  waiting for transfers between devices  243 us (38%)
  local copies, waits for them, and re-layouts  123 us (19%)
  other arithmetic  85.7 us (13%)
  starting transfers between devices  59.1 us (9%)
  Pallas kernels  55.1 us (9%)
  matrix products  49.2 us (8%)
  between operations  18.5 us (3%)
    psum x4, waiting for transfers between devices, scatter(): return lax.psum(part, 'ctx')  155 us
    unnamed x348, local copies, waits for them, and re-layouts  34.3 us
    ppermute x16, waiting for transfers between devices, reduce_rows(): got = lax.ppermute(sent, axis, partners(axis, bit)).astype(jnp.float32)  31.7 us
    ppermute x12, waiting for transfers between devices, gather_rows(): lax.ppermute(pieces[offset], axis, partners(axis, bit))  24.7 us
    ppermute x12, starting transfers between devices, shifted(): return lax.ppermute(values, 'ctx', pairs)  21.9 us
    pallas_call x1, Pallas kernels, attn_backward(): pl.pallas_call(partial(attn_bwd_kernel, heads), grid=(count // QUERY_ROWS...  17.8 us
    ppermute x16, starting transfers between devices, reduce_rows(): got = lax.ppermute(sent, axis, partners(axis, bit)).astype(jnp.float32)  17.5 us
    pallas_call x1, Pallas kernels, ssm_backward(): pl.pallas_call(partial(ssm_bwd_kernel, heads // 2), grid=(count // SPAN,)...  16 us
  transfers between devices with their start and end apart: 58, of which 20 were waited for; matrix products, arithmetic and copies ran while one was open for 36% of the time, Pallas kernels for 9%

profile of v2, /device:TPU:0, one launch (start us, length us, event | category | flops | bytes accessed | tf_op | source)
XLA Modules:
  0.0 633.7 jit_solution(16496874767481609544)
XLA Ops:
  34.6 12.0 %collective-permute-done.3 = bf16[128,2190]{0,1:T(8,128)(2,1)} collective-permute-done((bf16[128,2190]{0,1:T(8,128)(2,1)S(1)}, bf16[128,2190]{0,1:T(8,128)(2,1)}, u32[]{:S(2)}, u32[]{:S(2)}) %collective-permute-start.3) | collective-permute-done | bytes 560672 | tf_op jit(solution)/shard_map/ppermute | solution.py:117
  50.6 6.5 %collective-permute-done.2 = bf16[128,2190]{0,1:T(8,128)(2,1)S(1)} collective-permute-done((bf16[128,2190]{0,1:T(8,128)(2,1)}, bf16[128,2190]{0,1:T(8,128)(2,1)S(1)}, u32[]{:S(2)}, u32[]{:S(2)}) %collective-permute-start.2) | collective-permute-done | bytes 560672 | tf_op jit(solution)/shard_map/ppermute | solution.py:117
  68.2 5.0 fusion.123
  109.4 11.1 %attn_forward.1 = (f32[512,256]{1,0:T(8,128)S(1)}, f32[2048,1]{1,0:T(8,128)S(1)}) custom-call(bf16[512,256]{1,0:T(8,128)(2,1)S(1)} %copy-done.32, bf16[2048,128]{1,0:T(8,128)(2,1)S(1)} %constant_dynamic-update-slice_fusion.8.kv_ref, s32[512,1]{1,0:T(8,128)S(1)} %copy-done.25, s32[512,1]{1,0:T(8,128)S(1)} %copy-done.27), custom_call_target="tpu_custom_call" | custom-call | flops 1073741824 | bytes 524288 | tf_op jit(solution)/shard_map/attn_forward/pallas_call | solution.py:229
  130.5 7.1 %ssm_forward.1 = (f32[512,768]{1,0:T(8,128)S(1)}, f32[4,768,128]{2,1,0:T(8,128)S(1)}) custom-call(f32[512,768]{1,0:T(8,128)} %copy-done, bf16[512,128]{1,0:T(8,128)(2,1)S(1)} %get-tuple-element.353.m_ref.b_ref, bf16[512,128]{1,0:T(8,128)(2,1)S(1)} %get-tuple-element.352.c_ref.m_ref, f32[512,12]{1,0:T(8,128)S(1)} %get-tuple-element.287.step_ref, ...), custom_call_target="tpu_custom_call" | custom-call | tf_op jit(solution)/shard_map/ssm_forward/pallas_call | solution.py:447
  159.6 7.2 %fusion.98 = f32[512,2048]{1,0:T(8,128)} fusion(bf16[1024,2048]{1,0:T(8,128)(2,1)} %all-gather.3.cloned.1.call-done, f32[512,1024]{1,0:T(8,128)} %get-tuple-element.280, f32[1024]{0:T(1024)S(1)} %bitcast.290, f32[512]{0:T(512)S(1)} %get-tuple-element.379), kind=kOutput, calls=%fused_computation.346 | convolution fusion | flops 2149056512 | bytes 10491904 | tf_op jit(solution)/shard_map/dot_general | solution.py:669
  167.5 5.2 fusion.17
  177.6 4.5 convolution_convert_fusion.2
  213.7 4.3 subtract_add_fusion
  220.2 4.4 multiply_reduce_fusion.3
  224.8 17.8 %attn_backward.1 = (f32[512,256]{1,0:T(8,128)S(1)}, f32[2048,128]{1,0:T(8,128)S(1)}) custom-call(bf16[512,256]{1,0:T(8,128)(2,1)S(1)} %copy-done.33, bf16[2048,128]{1,0:T(8,128)(2,1)S(1)} %copy-done.24, s32[512,1]{1,0:T(8,128)S(1)} %copy-done.26, s32[512,1]{1,0:T(8,128)S(1)} %copy-done.28, f32[512,256]{1,0:T(8,128)S(1)} %copy-done.20, ...), custom_call_target="tpu_custom_call" | custom-call | flops 2684354560 | bytes 1048576 | tf_op jit(solution)/shard_map/attn_backward/pallas_call | solution.py:252
  280.3 8.5 %collective-permute-done.26 = bf16[784,128]{1,0:T(8,128)(2,1)} collective-permute-done((bf16[784,128]{1,0:T(8,128)(2,1)}, bf16[784,128]{1,0:T(8,128)(2,1)}, u32[]{:S(2)}, u32[]{:S(2)}) %collective-permute-start.26) | collective-permute-done | bytes 200736 | tf_op jit(solution)/shard_map/ppermute | solution.py:155
  293.4 16.0 %ssm_backward.1 = (f32[512,768]{1,0:T(8,128)S(1)}, f32[512,128]{1,0:T(8,128)S(1)}, f32[512,128]{1,0:T(8,128)S(1)}, f32[512,12]{1,0:T(8,128)S(1)}, f32[512,12]{1,0:T(8,128)S(1)}) custom-call(f32[512,768]{1,0:T(8,128)S(1)} %copy-done.1, bf16[512,128]{1,0:T(8,128)(2,1)S(1)} %copy-done.13, bf16[512,128]{1,0:T(8,128)(2,1)S(1)} %get-tuple-element.352.c_ref.m_ref, ...), custom_call_target="tpu_custom_call" | custom-call | tf_op jit(solution)/shard_map/ssm_backward/pallas_call | solution.py:466
  337.7 5.6 reshape.550
  348.7 4.6 copy.352
  355.6 4.7 copy.355
  379.1 13.6 %collective-permute-done.39 = bf16[128,1024]{0,1:T(8,128)(2,1)S(1)} collective-permute-done((bf16[128,1024]{0,1:T(8,128)(2,1)S(1)}, bf16[128,1024]{0,1:T(8,128)(2,1)S(1)}, u32[]{:S(2)}, u32[]{:S(2)}) %collective-permute-start.39) | collective-permute-done | bytes 262176 | tf_op jit(solution)/shard_map/ppermute | solution.py:139
  401.9 16.2 %collective-permute-done.35 = bf16[128,1152]{1,0:T(8,128)(2,1)S(1)} collective-permute-done((bf16[128,1152]{1,0:T(8,128)(2,1)}, bf16[128,1152]{1,0:T(8,128)(2,1)S(1)}, u32[]{:S(2)}, u32[]{:S(2)}) %collective-permute-start.35) | collective-permute-done | bytes 294944 | tf_op jit(solution)/shard_map/ppermute | solution.py:139
  437.3 6.6 %collective-permute-done.32 = f32[57,128]{1,0:T(8,128)S(1)} collective-permute-done((f32[57,128]{1,0:T(8,128)S(1)}, f32[57,128]{1,0:T(8,128)S(1)}, u32[]{:S(2)}, u32[]{:S(2)}) %collective-permute-start.32) | collective-permute-done | bytes 29216 | tf_op jit(solution)/shard_map/ppermute | solution.py:148
  444.8 5.0 collective-permute-done.33
  449.9 50.5 %all-reduce.24.cloned.1.call-done = bf16[256,3072]{0,1:T(8,128)(2,1)} async-done(((bf16[256,3072]{0,1:T(8,128)(2,1)}), bf16[256,3072]{0,1:T(8,128)(2,1)}) %all-reduce.24.cloned.1.call-update) | async-done | bytes 1572880 | tf_op jit(solution)/shard_map/psum | solution.py:694
  502.9 37.1 %all-reduce.26.cloned.1.call-done = bf16[256,1024]{0,1:T(8,128)(2,1)} async-done(((bf16[256,1024]{0,1:T(8,128)(2,1)}), bf16[256,1024]{0,1:T(8,128)(2,1)}) %all-reduce.26.cloned.1.call-update) | async-done | bytes 524304 | tf_op jit(solution)/shard_map/psum | solution.py:694
  549.5 32.4 %all-reduce.28.cloned.1.call-done = bf16[256,1152]{1,0:T(8,128)(2,1)} async-done(((bf16[256,1152]{1,0:T(8,128)(2,1)}), bf16[256,1152]{1,0:T(8,128)(2,1)}) %all-reduce.28.cloned.1.call-update) | async-done | bytes 589840 | tf_op jit(solution)/shard_map/psum | solution.py:694
  588.2 34.7 %all-reduce.30.cloned.1.call-done = bf16[256,1036]{0,1:T(8,128)(2,1)} async-done(((bf16[256,1036]{0,1:T(8,128)(2,1)}), bf16[256,1036]{0,1:T(8,128)(2,1)}) %all-reduce.30.cloned.1.call-update) | async-done | bytes 530448 | tf_op jit(solution)/shard_map/psum | solution.py:694
  (705 shorter events, 294.6 us)
Async XLA Ops:
  7.2 152.3 %all-gather.3.cloned.1.call-start = ((), (), s32[]{:S(2)}) async-start(), calls=%async_computation | async-start | bytes 5242880 | tf_op jit(solution)/shard_map/all_gather | solution.py:581
  18.9 29.7 %collective-permute-start.1 = (bf16[128,2190]{0,1:T(8,128)(2,1)S(1)}, bf16[128,2190]{0,1:T(8,128)(2,1)}, u32[]{:S(2)}, u32[]{:S(2)}) collective-permute-start(bf16[128,2190]{0,1:T(8,128)(2,1)S(1)} %get-tuple-element.328), channel_id=1, source_target_pairs={{0,8},{8,0},{16,24},{24,16},{1,9},{9,1},{17,25},{25,17},{2,10},{10... | collective-permute-start | bytes 1681928 | tf_op jit(solution)/shard_map/ppermute | solution.py:117
  20.9 40.0 %collective-permute-start.4 = (bf16[128,2190]{0,1:T(8,128)(2,1)S(1)}, bf16[128,2190]{0,1:T(8,128)(2,1)}, u32[]{:S(2)}, u32[]{:S(2)}) collective-permute-start(bf16[128,2190]{0,1:T(8,128)(2,1)S(1)} %get-tuple-element.326), channel_id=1, source_target_pairs={{0,16},{8,24},{16,0},{24,8},{1,17},{9,25},{17,1},{25,9},{2,18},{10... | collective-permute-start | bytes 1681928 | tf_op jit(solution)/shard_map/ppermute | solution.py:117
  63.8 103.7 %all-gather.5.cloned.1.call-start = ((), (), s32[]{:S(2)}) async-start(), calls=%async_computation.1 | async-start | bytes 2621440 | tf_op jit(solution)/shard_map/all_gather | solution.py:582
  92.9 44.8 %collective-permute-start.13 = (bf16[128,1024]{0,1:T(8,128)(2,1)}, bf16[128,1024]{0,1:T(8,128)(2,1)}, u32[]{:S(2)}, u32[]{:S(2)}) collective-permute-start(bf16[128,1024]{0,1:T(8,128)(2,1)} %get-tuple-element.346), channel_id=1, source_target_pairs={{0,16},{8,24},{16,0},{24,8},{1,17},{9,25},{17,1},{25,9},{2,18},{10... | collective-permute-start | bytes 786440 | tf_op jit(solution)/shard_map/ppermute | solution.py:117
  93.5 406.8 %all-reduce.24.cloned.1.call-start = ((), (), s32[]{:S(2)}) async-start(), calls=%async_computation.2 | async-start | bytes 3145728 | tf_op jit(solution)/shard_map/psum | solution.py:694
  96.2 47.4 %collective-permute-start.14 = (bf16[128,1024]{0,1:T(8,128)(2,1)}, bf16[128,1024]{0,1:T(8,128)(2,1)}, u32[]{:S(2)}, u32[]{:S(2)}) collective-permute-start(bf16[128,1024]{0,1:T(8,128)(2,1)} %get-tuple-element.346), channel_id=1, source_target_pairs={{0,8},{8,0},{16,24},{24,16},{1,9},{9,1},{17,25},{25,17},{2,10},{10... | collective-permute-start | bytes 786440 | tf_op jit(solution)/shard_map/ppermute | solution.py:117
  104.2 37.6 %collective-permute-start.16 = (bf16[128,1024]{0,1:T(8,128)(2,1)}, bf16[128,1024]{0,1:T(8,128)(2,1)}, u32[]{:S(2)}, u32[]{:S(2)}) collective-permute-start(bf16[128,1024]{0,1:T(8,128)(2,1)} %get-tuple-element.344), channel_id=1, source_target_pairs={{0,8},{8,0},{16,24},{24,16},{1,9},{9,1},{17,25},{25,17},{2,10},{10... | collective-permute-start | bytes 786440 | tf_op jit(solution)/shard_map/ppermute | solution.py:117
  122.3 26.9 %collective-permute-start.17 = (bf16[128,1024]{0,1:T(8,128)(2,1)}, bf16[128,1024]{0,1:T(8,128)(2,1)}, u32[]{:S(2)}, u32[]{:S(2)}) collective-permute-start(bf16[128,1024]{0,1:T(8,128)(2,1)} %get-tuple-element.344), channel_id=1, source_target_pairs={{0,16},{8,24},{16,0},{24,8},{1,17},{9,25},{17,1},{25,9},{2,18},{10... | collective-permute-start | bytes 786440 | tf_op jit(solution)/shard_map/ppermute | solution.py:117
  177.6 36.1 %collective-permute-start.20 = (bf16[512,1024]{1,0:T(8,128)(2,1)}, bf16[512,1024]{1,0:T(8,128)(2,1)}, u32[]{:S(2)}, u32[]{:S(2)}) collective-permute-start(bf16[512,1024]{1,0:T(8,128)(2,1)} %convolution_convert_fusion.6), channel_id=1, source_target_pairs={{0,1},{1,0},{2,3},{3,2},{4,5},{5,4},{6,7},{7,6},{8,9},{9,8},{10,11... | collective-permute-start | bytes 3145736 | tf_op jit(solution)/shard_map/ppermute | solution.py:92
  196.5 163.8 %collective-permute-start.42 = (bf16[2,128,3072]{1,2,0:T(8,128)(2,1)}, bf16[2,128,3072]{1,2,0:T(8,128)(2,1)}, u32[]{:S(2)}, u32[]{:S(2)}) collective-permute-start(bf16[2,128,3072]{1,2,0:T(8,128)(2,1)} %bitcast.283), channel_id=1, source_target_pairs={{0,16},{8,24},{16,0},{24,8},{1,17},{9,25},{17,1},{25,9},{2,18},{10... | collective-permute-start | bytes 4718600 | tf_op jit(solution)/shard_map/ppermute | solution.py:139
  206.9 156.8 %collective-permute-start.44 = (bf16[2,128,3072]{1,2,0:T(8,128)(2,1)}, bf16[2,128,3072]{1,2,0:T(8,128)(2,1)}, u32[]{:S(2)}, u32[]{:S(2)}) collective-permute-start(bf16[2,128,3072]{1,2,0:T(8,128)(2,1)} %bitcast.284), channel_id=1, source_target_pairs={{0,8},{8,0},{16,24},{24,16},{1,9},{9,1},{17,25},{25,17},{2,10},{10... | collective-permute-start | bytes 4718600 | tf_op jit(solution)/shard_map/ppermute | solution.py:139
  278.8 87.4 %collective-permute-start.38 = (bf16[2,128,1024]{1,2,0:T(8,128)(2,1)}, bf16[2,128,1024]{1,2,0:T(8,128)(2,1)}, u32[]{:S(2)}, u32[]{:S(2)}) collective-permute-start(bf16[2,128,1024]{1,2,0:T(8,128)(2,1)} %bitcast.53), channel_id=1, source_target_pairs={{0,16},{8,24},{16,0},{24,8},{1,17},{9,25},{17,1},{25,9},{2,18},{10... | collective-permute-start | bytes 1572872 | tf_op jit(solution)/shard_map/ppermute | solution.py:139
  288.8 80.3 %collective-permute-start.40 = (bf16[2,128,1024]{1,2,0:T(8,128)(2,1)}, bf16[2,128,1024]{1,2,0:T(8,128)(2,1)}, u32[]{:S(2)}, u32[]{:S(2)}) collective-permute-start(bf16[2,128,1024]{1,2,0:T(8,128)(2,1)} %bitcast.57), channel_id=1, source_target_pairs={{0,8},{8,0},{16,24},{24,16},{1,9},{9,1},{17,25},{25,17},{2,10},{10... | collective-permute-start | bytes 1572872 | tf_op jit(solution)/shard_map/ppermute | solution.py:139
  333.3 39.4 %collective-permute-start.34 = (bf16[2,128,1152]{2,1,0:T(8,128)(2,1)}, bf16[2,128,1152]{2,1,0:T(8,128)(2,1)}, u32[]{:S(2)}, u32[]{:S(2)}) collective-permute-start(bf16[2,128,1152]{2,1,0:T(8,128)(2,1)} %dynamic-slice_bitcast_fusion.3), channel_id=1, source_target_pairs={{0,16},{8,24},{16,0},{24,8},{1,17},{9,25},{17,1},{25,9},{2,18},{10... | collective-permute-start | bytes 1769480 | tf_op jit(solution)/shard_map/ppermute | solution.py:139
  363.7 57.5 %collective-permute-start.29 = (bf16[512,1024]{1,0:T(8,128)(2,1)}, bf16[512,1024]{1,0:T(8,128)(2,1)}, u32[]{:S(2)}, u32[]{:S(2)}) collective-permute-start(bf16[512,1024]{1,0:T(8,128)(2,1)} %add_convert_fusion), channel_id=1, source_target_pairs={{0,1},{1,0},{2,3},{3,2},{4,5},{5,4},{6,7},{7,6},{8,9},{9,8},{10,11... | collective-permute-start | bytes 3145736 | tf_op jit(solution)/shard_map/ppermute | solution.py:92
  366.2 29.6 %collective-permute-start.47 = (bf16[2,128,1036]{1,0,2:T(2,128)(2,1)}, bf16[2,128,1036]{1,0,2:T(2,128)(2,1)}, u32[]{:S(2)}, u32[]{:S(2)}) collective-permute-start(bf16[2,128,1036]{1,0,2:T(2,128)(2,1)} %copy.352), channel_id=1, source_target_pairs={{0,16},{8,24},{16,0},{24,8},{1,17},{9,25},{17,1},{25,9},{2,18},{10... | collective-permute-start | bytes 1591304 | tf_op jit(solution)/shard_map/ppermute | solution.py:139
  369.1 29.5 %collective-permute-start.49 = (bf16[2,128,1036]{1,0,2:T(2,128)(2,1)}, bf16[2,128,1036]{1,0,2:T(2,128)(2,1)}, u32[]{:S(2)}, u32[]{:S(2)}) collective-permute-start(bf16[2,128,1036]{1,0,2:T(2,128)(2,1)} %copy.355), channel_id=1, source_target_pairs={{0,8},{8,0},{16,24},{24,16},{1,9},{9,1},{17,25},{25,17},{2,10},{10... | collective-permute-start | bytes 1591304 | tf_op jit(solution)/shard_map/ppermute | solution.py:139
  392.8 35.9 %collective-permute-start.43 = (bf16[128,3072]{0,1:T(8,128)(2,1)}, bf16[128,3072]{0,1:T(8,128)(2,1)}, u32[]{:S(2)}, u32[]{:S(2)}) collective-permute-start(bf16[128,3072]{0,1:T(8,128)(2,1)} %dynamic-slice_bitcast_fusion.1), channel_id=1, source_target_pairs={{0,8},{8,0},{16,24},{24,16},{1,9},{9,1},{17,25},{25,17},{2,10},{10... | collective-permute-start | bytes 2359304 | tf_op jit(solution)/shard_map/ppermute | solution.py:139
  394.3 35.9 %collective-permute-start.45 = (bf16[128,3072]{0,1:T(8,128)(2,1)}, bf16[128,3072]{0,1:T(8,128)(2,1)}, u32[]{:S(2)}, u32[]{:S(2)}) collective-permute-start(bf16[128,3072]{0,1:T(8,128)(2,1)} %dynamic-slice_bitcast_fusion), channel_id=1, source_target_pairs={{0,16},{8,24},{16,0},{24,8},{1,17},{9,25},{17,1},{25,9},{2,18},{10... | collective-permute-start | bytes 2359304 | tf_op jit(solution)/shard_map/ppermute | solution.py:139
  433.1 106.9 %all-reduce.26.cloned.1.call-start = ((), (), s32[]{:S(2)}) async-start(), calls=%async_computation.3 | async-start | bytes 1048576 | tf_op jit(solution)/shard_map/psum | solution.py:694
  449.8 90.2 %collective-permute-start.51 = (f32[10,128]{1,0:T(8,128)S(1)}, f32[10,128]{1,0:T(8,128)S(1)}, u32[]{:S(2)}, u32[]{:S(2)}) collective-permute-start(f32[10,128]{1,0:T(8,128)S(1)} %slice.714), channel_id=1, source_target_pairs={{0,1},{1,0},{2,3},{3,2},{4,5},{5,4},{6,7},{7,6},{8,9},{9,8},{10,11... | collective-permute-start | bytes 15368 | tf_op jit(solution)/shard_map/ppermute | solution.py:148
  500.4 81.4 %all-reduce.28.cloned.1.call-start = ((), (), s32[]{:S(2)}) async-start(), calls=%async_computation.4 | async-start | bytes 1179648 | tf_op jit(solution)/shard_map/psum | solution.py:694
  540.0 82.9 %all-reduce.30.cloned.1.call-start = ((), (), s32[]{:S(2)}) async-start(), calls=%async_computation.5 | async-start | bytes 1064960 | tf_op jit(solution)/shard_map/psum | solution.py:694
  (194 other events, 2434.3 us)
Sparse Core Ops, SparseCore 0:
  63.9 64.2 all-gather.2
  130.0 37.4 all-gather.4
  433.2 67.1 all-reduce.23
  502.6 37.3 all-reduce.25
  542.7 39.0 all-reduce.27
  584.6 38.1 all-reduce.29
